TPU v7x, 32 devices: a whole 2x2x4 slice. The times are simulated.
32 devices in a mesh: dp: 4 (over y, x), seq: 8 (over z, core).
Axes of the slice: x: 2, y: 2, z: 4, core: 2. Of those that a mesh axis runs over, the one named last changes fastest.
Arguments:
- tokens: bfloat16 [12, 1024, 512], P('dp', 'seq'), may hold values from -6 to 6
- grad_out: bfloat16 [12, 1024, 512], P('dp', 'seq'), may hold values from -6 to 6
- crop: int32 [12], P('dp'), may hold values from 512 to 1024
- offsets: int32 [12, 4], P('dp'), may hold values from 0 to 1023, as said below
- w_query: bfloat16 [512, 512], replicated, may hold values from -0.25 to 0.25
- w_key: bfloat16 [512, 512], replicated, may hold values from -0.25 to 0.25
- w_value: bfloat16 [512, 512], replicated, may hold values from -0.25 to 0.25
- w_out: bfloat16 [512, 512], replicated, may hold values from -6 to 6
- w_up: bfloat16 [512, 2048], replicated, may hold values from -0.25 to 0.25
- w_down: bfloat16 [2048, 512], replicated, may hold values from -0.125 to 0.125
- b_query: float32 [512], replicated, may hold values from -3 to 3
- b_value: float32 [512], replicated, may hold values from -3 to 3
- b_out: float32 [512], replicated, may hold values from -3 to 3
- b_up: float32 [2048], replicated, may hold values from -3 to 3
- b_down: float32 [512], replicated, may hold values from -3 to 3
- gain_one: float32 [512], replicated, may hold values from 0.5 to 1.5
- shift_one: float32 [512], replicated, may hold values from -3 to 3
- gain_two: float32 [512], replicated, may hold values from 0.5 to 1.5
- shift_two: float32 [512], replicated, may hold values from -3 to 3
Outputs:
- activations: bfloat16 [12, 1024, 512], P('dp', 'seq')
- input_grad: bfloat16 [12, 1024, 512], P('dp', 'seq')
- grad_w_query: float32 [512, 512], replicated
- grad_w_key: float32 [512, 512], replicated
- grad_w_value: float32 [512, 512], replicated
- grad_w_out: float32 [512, 512], replicated
- grad_w_up: float32 [512, 2048], replicated
- grad_w_down: float32 [2048, 512], replicated
- grad_b_query: float32 [512], replicated
- grad_b_value: float32 [512], replicated
- grad_b_out: float32 [512], replicated
- grad_b_up: float32 [2048], replicated
- grad_b_down: float32 [512], replicated
- grad_gain_one: float32 [512], replicated
- grad_shift_one: float32 [512], replicated
- grad_gain_two: float32 [512], replicated
- grad_shift_two: float32 [512], replicated
Inputs may be any that keep to these rules, and one draw needn't show every extreme that they name: offsets[r, 0] is 0, a row's offsets do not fall, and each stays below crop[r].
All inputs are finite; a program needn't handle non-finite values.
Results may differ from a plain program's by a relative error of at most 0.013.
Values may be sent and summed in bfloat16 or wider, within the bound.
No kernel may reach another device: no remote copies, remote signals or barrier semaphores. Data moves between devices by JAX's collectives and lax.ppermute only.
A program may use at most 192 MiB of HBM per device.

v0:
```python
import jax
import jax.numpy as jnp
from jax import lax
from jax.sharding import PartitionSpec as P

HEADS = 8


EPSILON = 1e-06
MASKED = -1e30


def passed_along(block, axis, distance):
    devices = range(lax.axis_size(axis))
    route = [((i - distance) % len(devices), i) for i in devices]
    return lax.ppermute(block, axis, route)


def layer_norm(values, gain, shift):
    center = values - jnp.mean(values, axis=-1, keepdims=True)
    spread = jnp.mean(center * center, axis=-1, keepdims=True)
    return center * lax.rsqrt(spread + EPSILON) * gain + shift


def gelu_tanh(values):
    return jax.nn.gelu(values, approximate=True)


def segment_index(positions, offsets, crop):
    after = (positions[None, :, None] >= offsets[:, None, :]).astype(jnp.int32)
    padded = (positions[None, :] >= crop[:, None]).astype(jnp.int32)
    return jnp.sum(after, axis=-1, dtype=jnp.int32) + offsets.shape[1] * padded


def split_heads(values):
    return values.reshape(values.shape[0], values.shape[1], HEADS, values.shape[2] // HEADS)


def merge_heads(values):
    return values.reshape(values.shape[0], values.shape[1], values.shape[2] * values.shape[3])


def block_scores(query_rows, key_rows, query_seg, key_seg, score_scale):
    scores = (
        jnp.einsum("rqhe,rkhe->rhqk", query_rows, key_rows, preferred_element_type=jnp.float32)
        * score_scale
    )
    allowed = query_seg[:, None, :, None] == key_seg[:, None, None, :]
    return (scores, allowed)


def attend_back(
    query_rows,
    out_grad,
    log_total,
    delta_rows,
    query_seg,
    key_rows,
    value_rows,
    key_seg,
    score_scale,
):
    scores, allowed = block_scores(query_rows, key_rows, query_seg, key_seg, score_scale)
    probs = jnp.where(allowed, jnp.exp(scores - log_total[..., None]), 0.0)
    prob_grad = jnp.einsum(
        "rqhe,rkhe->rhqk", out_grad, value_rows, preferred_element_type=jnp.float32
    )
    score_grad = (probs * (prob_grad - delta_rows[..., None])).astype(jnp.bfloat16)
    query_add = (
        jnp.einsum("rhqk,rkhe->rqhe", score_grad, key_rows, preferred_element_type=jnp.float32)
        * score_scale
    )
    key_add = (
        jnp.einsum("rhqk,rqhe->rkhe", score_grad, query_rows, preferred_element_type=jnp.float32)
        * score_scale
    )
    value_add = jnp.einsum(
        "rhqk,rqhe->rkhe", probs.astype(jnp.bfloat16), out_grad, preferred_element_type=jnp.float32
    )
    return (merge_heads(query_add), merge_heads(key_add), merge_heads(value_add))


def body(
    tokens,
    grad_out,
    crop,
    offsets,
    w_query,
    w_key,
    w_value,
    w_out,
    w_up,
    w_down,
    b_query,
    b_value,
    b_out,
    b_up,
    b_down,
    gain_one,
    shift_one,
    gain_two,
    shift_two,
):
    row_count, tok_count, model_width = tokens.shape
    head_size = model_width // HEADS
    score_scale = head_size ** (-0.5)
    seq_count = lax.axis_size("seq")
    my_index = lax.axis_index("seq")
    flat_rows = row_count * tok_count
    row_shape = (row_count, tok_count, model_width)

    def block_segments(block_number):
        return segment_index(
            block_number * tok_count + jnp.arange(tok_count, dtype=jnp.int32), offsets, crop
        )

    own_segments = block_segments(my_index)
    token_float = tokens.astype(jnp.float32).reshape(flat_rows, model_width)
    normed_one = layer_norm(token_float, gain_one, shift_one).astype(jnp.bfloat16)
    query_low = (
        (jnp.dot(normed_one, w_query, preferred_element_type=jnp.float32) + b_query)
        .astype(jnp.bfloat16)
        .reshape(row_shape)
    )
    key_low = (
        jnp.dot(normed_one, w_key, preferred_element_type=jnp.float32)
        .astype(jnp.bfloat16)
        .reshape(row_shape)
    )
    value_low = (
        (jnp.dot(normed_one, w_value, preferred_element_type=jnp.float32) + b_value)
        .astype(jnp.bfloat16)
        .reshape(row_shape)
    )
    query_heads = split_heads(query_low)
    stat_shape = (row_count, HEADS, tok_count)
    piece = lax.all_gather(key_low, "seq", axis=1, tiled=True)
    running_max = jnp.full(stat_shape, MASKED, jnp.float32)
    piece_seg = segment_index(jnp.arange(piece.shape[1], dtype=jnp.int32), offsets, crop)
    scores, allowed = block_scores(
        query_heads, split_heads(piece), own_segments, piece_seg, score_scale
    )
    scores = jnp.where(allowed, scores, MASKED)
    new_max = jnp.maximum(running_max, jnp.max(scores, axis=-1))
    weights = jnp.where(allowed, jnp.exp(scores - new_max[..., None]), 0.0)
    score_total = jnp.sum(weights, axis=-1)
    log_total = new_max + jnp.log(score_total)
    key_piece = lax.all_gather(key_low, "seq", axis=1, tiled=True)
    value_piece = lax.all_gather(value_low, "seq", axis=1, tiled=True)
    piece_seg = segment_index(jnp.arange(key_piece.shape[1], dtype=jnp.int32), offsets, crop)
    scores, allowed = block_scores(
        query_heads, split_heads(key_piece), own_segments, piece_seg, score_scale
    )
    weights = jnp.where(allowed, jnp.exp(scores - log_total[..., None]), 0.0).astype(jnp.bfloat16)
    added = jnp.einsum(
        "rhqk,rkhe->rqhe", weights, split_heads(value_piece), preferred_element_type=jnp.float32
    )
    attended = merge_heads(added)
    attended_low = attended.astype(jnp.bfloat16).reshape(flat_rows, model_width)
    mid_stream = (
        token_float + jnp.dot(attended_low, w_out, preferred_element_type=jnp.float32) + b_out
    )
    normed_two = layer_norm(mid_stream, gain_two, shift_two).astype(jnp.bfloat16)
    hidden_pre = jnp.dot(normed_two, w_up, preferred_element_type=jnp.float32) + b_up
    hidden_low = gelu_tanh(hidden_pre).astype(jnp.bfloat16)
    outputs = mid_stream + jnp.dot(hidden_low, w_down, preferred_element_type=jnp.float32) + b_down
    outputs = outputs.astype(jnp.bfloat16).reshape(row_shape)
    cotangent = grad_out.reshape(flat_rows, model_width)
    cotangent_float = cotangent.astype(jnp.float32)
    grad_down = jnp.dot(hidden_low.T, cotangent, preferred_element_type=jnp.float32)
    bias_down = jnp.sum(cotangent_float, axis=0)
    hidden_grad = jnp.dot(cotangent, w_down.T, preferred_element_type=jnp.float32)
    _, gelu_back = jax.vjp(gelu_tanh, hidden_pre)
    pre_grad = gelu_back(hidden_grad)[0].astype(jnp.bfloat16)
    grad_up = jnp.dot(normed_two.T, pre_grad, preferred_element_type=jnp.float32)
    bias_up = jnp.sum(pre_grad.astype(jnp.float32), axis=0)
    normed_two_grad = jnp.dot(pre_grad, w_up.T, preferred_element_type=jnp.float32)
    _, norm_two_back = jax.vjp(layer_norm, mid_stream, gain_two, shift_two)
    mid_part, gain_two_grad, shift_two_grad = norm_two_back(normed_two_grad)
    mid_grad = cotangent_float + mid_part
    branch_low = mid_grad.astype(jnp.bfloat16)
    grad_out_proj = jnp.dot(attended_low.T, branch_low, preferred_element_type=jnp.float32)
    bias_out = jnp.sum(branch_low.astype(jnp.float32), axis=0)
    attended_grad = (
        jnp.dot(branch_low, w_out.T, preferred_element_type=jnp.float32)
        .astype(jnp.bfloat16)
        .reshape(row_shape)
    )
    delta_rows = jnp.einsum(
        "rqhe,rqhe->rhq", split_heads(attended_grad).astype(jnp.float32), split_heads(attended)
    )
    grad_heads = split_heads(attended_grad)
    zero_rows = jnp.zeros(row_shape, jnp.float32)

    def key_turn(turn_index, carry):
        query_grad, key_rows, value_rows, key_grad, value_grad = carry
        held_seg = block_segments((my_index + turn_index) % seq_count)
        query_add, key_add, value_add = attend_back(
            query_heads,
            grad_heads,
            log_total,
            delta_rows,
            own_segments,
            split_heads(key_rows),
            split_heads(value_rows),
            held_seg,
            score_scale,
        )
        key_rows, value_rows = passed_along((key_rows, value_rows), "seq", -1)
        key_grad, value_grad = (
            passed_along((key_grad + key_add).astype(jnp.bfloat16), "seq", -1).astype(jnp.float32),
            passed_along((value_grad + value_add).astype(jnp.bfloat16), "seq", -1).astype(
                jnp.float32
            ),
        )
        return (query_grad + query_add, key_rows, value_rows, key_grad, value_grad)

    query_grad, key_rows, value_rows, key_grad, value_grad = lax.fori_loop(
        0, seq_count - 1, key_turn, (zero_rows, key_low, value_low, zero_rows, zero_rows)
    )
    last_seg = block_segments((my_index + seq_count - 1) % seq_count)
    query_add, key_add, value_add = attend_back(
        query_heads,
        grad_heads,
        log_total,
        delta_rows,
        own_segments,
        split_heads(key_rows),
        split_heads(value_rows),
        last_seg,
        score_scale,
    )
    query_grad = query_grad + query_add
    key_grad, value_grad = (
        passed_along((key_grad + key_add).astype(jnp.bfloat16), "seq", -1).astype(jnp.float32),
        passed_along((value_grad + value_add).astype(jnp.bfloat16), "seq", -1).astype(jnp.float32),
    )
    query_grad_low = query_grad.astype(jnp.bfloat16).reshape(flat_rows, model_width)
    key_grad_low = key_grad.astype(jnp.bfloat16).reshape(flat_rows, model_width)
    value_grad_low = value_grad.astype(jnp.bfloat16).reshape(flat_rows, model_width)
    grad_query = jnp.dot(normed_one.T, query_grad_low, preferred_element_type=jnp.float32)
    grad_key = jnp.dot(normed_one.T, key_grad_low, preferred_element_type=jnp.float32)
    grad_value = jnp.dot(normed_one.T, value_grad_low, preferred_element_type=jnp.float32)
    bias_query = jnp.sum(query_grad_low.astype(jnp.float32), axis=0)
    bias_value = jnp.sum(value_grad_low.astype(jnp.float32), axis=0)
    normed_one_grad = (
        jnp.dot(query_grad_low, w_query.T, preferred_element_type=jnp.float32)
        + jnp.dot(key_grad_low, w_key.T, preferred_element_type=jnp.float32)
        + jnp.dot(value_grad_low, w_value.T, preferred_element_type=jnp.float32)
    )
    _, norm_one_back = jax.vjp(layer_norm, token_float, gain_one, shift_one)
    token_part, gain_one_grad, shift_one_grad = norm_one_back(normed_one_grad)
    input_grad = (mid_grad + token_part).astype(jnp.bfloat16).reshape(row_shape)
    summed = lax.psum(
        (
            grad_query,
            grad_key,
            grad_value,
            grad_out_proj,
            grad_up,
            grad_down,
            bias_query,
            bias_value,
            bias_out,
            bias_up,
            bias_down,
            gain_one_grad,
            shift_one_grad,
            gain_two_grad,
            shift_two_grad,
        ),
        ("dp", "seq"),
    )
    return (outputs, input_grad) + tuple(summed)


def solution(mesh):
    return jax.shard_map(
        body,
        mesh=mesh,
        in_specs=(
            P("dp", "seq", None),
            P("dp", "seq", None),
            P("dp"),
            P("dp", None),
            P(),
            P(),
            P(),
            P(),
            P(),
            P(),
            P(),
            P(),
            P(),
            P(),
            P(),
            P(),
            P(),
            P(),
            P(),
        ),
        out_specs=(
            P("dp", "seq", None),
            P("dp", "seq", None),
            P(),
            P(),
            P(),
            P(),
            P(),
            P(),
            P(),
            P(),
            P(),
            P(),
            P(),
            P(),
            P(),
            P(),
            P(),
        ),
        check_vma=False,
    )
```

profile of v0, /device:TPU:0, one launch (start us, length us, event | category | flops | bytes accessed | tf_op | source)
XLA Modules:
  0.0 583.5 jit_solution(1408900562678676663)
XLA Ops:
  25.9 4.4 fusion.40
  30.3 24.1 %all-gather.5.cloned.1.call-done = bf16[3,1024,512]{2,1,0:T(8,128)(2,1)} async-done(((bf16[3,128,512]{2,1,0:T(8,128)(2,1)}), bf16[3,1024,512]{2,1,0:T(8,128)(2,1)}) %all-gather.5.cloned.1.call-update) | async-done | bytes 3145744 | tf_op jit(solution)/shard_map/all_gather | solution.py:148
  54.4 4.6 copy.80
  59.0 4.4 select_reduce_fusion.1
  63.5 3.9 select_reduce_fusion
  68.0 25.8 %all-gather.3.cloned.1.call-done = bf16[3,1024,512]{2,1,0:T(8,128)(2,1)} async-done(((bf16[3,128,512]{2,1,0:T(8,128)(2,1)}), bf16[3,1024,512]{2,1,0:T(8,128)(2,1)}) %all-gather.3.cloned.1.call-update) | async-done | bytes 3145744 | tf_op jit(solution)/shard_map/all_gather | solution.py:149
  93.8 4.6 copy.78
  98.4 9.2 %bitcast_convert_fusion = (bf16[3,128,8,64]{1,3,2,0:T(8,128)(2,1)S(1)}, f32[3,8,64,128]{3,2,1,0:T(8,128)}) fusion(bf16[3,1024,8,64]{1,3,2,0:T(8,128)(2,1)} %bitcast.179, f32[3,8,128,1024]{3,2,1,0:T(8,128)} %copy-done.2, f32[3,8,128]{2,1,0:T(8,128)S(1)} %log_add_fusion, pred[3,128,1024]{2,1,0:T(8,128)(4,1)} %broadcast_compare_fusion.1), kind=kOutput, calls=%fused_computation.56 | convolution fusion | flops 415432704 | bytes 17313792 | tf_op jit(solution)/shard_map/rhqk,rkhe->rqhe/dot_general | solution.py:155
  109.9 4.5 convert_reduce_fusion.1
  118.8 164.3 %while.24 = (s32[]{:T(128)}, f32[3,128,512]{1,2,0:T(8,128)}, bf16[3,128,512]{1,2,0:T(8,128)(2,1)}, bf16[3,128,512]{1,2,0:T(8,128)(2,1)}, f32[3,128,512]{1,2,0:T(...) while((s32[]{:T(128)}, f32[3,128,512]{1,2,0:T(8,128)}, ...), condition=%wide.region_12.13_spmd.clone, body=%wide.region_10.0_spmd.clone.sunk | while | flops 256824720 | bytes 31983160 | solution.py:218
  129.7 5.2 collective-permute-done.2
  141.1 3.7 collective-permute-start
  152.8 5.8 collective-permute-done.2
  164.9 3.7 collective-permute-start
  176.7 5.8 collective-permute-done.2
  188.8 3.7 collective-permute-start
  200.5 5.8 collective-permute-done.2
  212.6 3.7 collective-permute-start
  224.3 5.8 collective-permute-done.2
  236.4 3.7 collective-permute-start
  248.2 5.8 collective-permute-done.2
  260.3 3.7 collective-permute-start
  272.0 5.8 collective-permute-done.2
  289.2 2.5 convolution_multiply_fusion.3
  291.7 3.4 fusion.33
  297.7 5.5 fusion.34
  309.7 4.0 collective-permute-start.4
  320.5 2.6 collective-permute-done.5
  328.0 4.5 fusion.17
  334.7 41.0 %all-reduce = (f32[512]{0:T(512)}, f32[512]{0:T(512)}, f32[512]{0:T(512)}, f32[2048]{0:T(1024)}, f32[512]{0:T(512)}, /*index=5*/f32[512]{0:T(512)}, f32[512]{0:T(512)}, f32[512]{0:T(512)}, f32[512]{0:T(512)}) all-reduce(f32[512]{0:T(512)S(1)} %get-tuple-element.500, ...), channel_id=1, replica_groups=mesh['dp'=4,'seq'=8] {'dp','seq'}, use_global_device_ids=true, to_apply=%region_23.24 | all-reduce | flops 6144 | bytes 49152 | tf_op jit(solution)/shard_map/psum | solution.py:254
  376.9 187.6 %all-reduce.4.cloned.1.call-done = (f32[512,512]{1,0:T(8,128)}, f32[512,512]{1,0:T(8,128)}, f32[512,512]{1,0:T(8,128)}, f32[512,512]{1,0:T(8,128)}, f32[512,2048]{1,0:T(8,128)}, /*index=5*/f32[2048,512]{1,0:T(8,128)}) async-done(((f32[512,512]{1,0:T(8,128)}, f32[512,512]{1,0:T(8,128)}, f32[512,512]{1,0:T(8,128)}, f32[512,512]{1,0:T(8,128)}, f32[512,2048]{1,0:T(8,128)}, /*index=5*/f32[2048,512]{1,0:T(8,128)}), ...) | async-done | bytes 12582928 | tf_op jit(solution)/shard_map/psum | solution.py:254
  566.9 2.4 copy.149
  (345 shorter events, 167.5 us)
Async XLA Ops:
  7.2 47.2 %all-gather.5.cloned.1.call-start = ((), (), s32[]{:S(2)}) async-start(), calls=%async_computation.1 | async-start | bytes 3538944 | tf_op jit(solution)/shard_map/all_gather | solution.py:148
  13.3 80.5 %all-gather.3.cloned.1.call-start = ((), (), s32[]{:S(2)}) async-start(), calls=%async_computation | async-start | bytes 3538944 | tf_op jit(solution)/shard_map/all_gather | solution.py:149
  14.5 550.0 %all-reduce.4.cloned.1.call-start = ((), (), s32[]{:S(2)}) async-start(), calls=%async_computation.2 | async-start | bytes 25165824 | tf_op jit(solution)/shard_map/psum | solution.py:254
  119.8 20.3 %collective-permute-start = (bf16[3,128,512]{1,2,0:T(8,128)(2,1)S(1)}, bf16[3,128,512]{1,2,0:T(8,128)(2,1)}, u32[]{:S(2)}, u32[]{:S(2)}) collective-permute-start(bf16[3,128,512]{1,2,0:T(8,128)(2,1)S(1)} %copy.132), channel_id=1, source_target_pairs={{1,0},{2,1},{3,2},{4,3},{5,4},{6,5},{7,6},{0,7},{9,8},{10,9},{11,1... | collective-permute-start | bytes 1179656 | tf_op jit(solution)/shard_map/while/body/eval_jaxpr/ppermute | solution.py:16
  122.0 18.1 %collective-permute-start.1 = (bf16[3,128,512]{1,2,0:T(8,128)(2,1)S(1)}, bf16[3,128,512]{1,2,0:T(8,128)(2,1)}, u32[]{:S(2)}, u32[]{:S(2)}) collective-permute-start(bf16[3,128,512]{1,2,0:T(8,128)(2,1)S(1)} %copy.133), channel_id=1, source_target_pairs={{1,0},{2,1},{3,2},{4,3},{5,4},{6,5},{7,6},{0,7},{9,8},{10,9},{11,1... | collective-permute-start | bytes 1179656 | tf_op jit(solution)/shard_map/while/body/eval_jaxpr/ppermute | solution.py:16
  125.3 9.5 %collective-permute-start.2 = (bf16[3,128,512]{1,2,0:T(8,128)(2,1)}, bf16[3,128,512]{1,2,0:T(8,128)(2,1)}, u32[]{:S(2)}, u32[]{:S(2)}) collective-permute-start(bf16[3,128,512]{1,2,0:T(8,128)(2,1)} %fusion.113), channel_id=1, source_target_pairs={{1,0},{2,1},{3,2},{4,3},{5,4},{6,5},{7,6},{0,7},{9,8},{10,9},{11,1... | collective-permute-start | bytes 1179656 | tf_op jit(solution)/shard_map/while/body/eval_jaxpr/ppermute | solution.py:16
  127.7 11.3 %collective-permute-start.3 = (bf16[3,128,512]{1,2,0:T(8,128)(2,1)}, bf16[3,128,512]{1,2,0:T(8,128)(2,1)}, u32[]{:S(2)}, u32[]{:S(2)}) collective-permute-start(bf16[3,128,512]{1,2,0:T(8,128)(2,1)} %fusion.115), channel_id=1, source_target_pairs={{1,0},{2,1},{3,2},{4,3},{5,4},{6,5},{7,6},{0,7},{9,8},{10,9},{11,1... | collective-permute-start | bytes 1179656 | tf_op jit(solution)/shard_map/while/body/eval_jaxpr/ppermute | solution.py:16
  141.1 22.8 %collective-permute-start = (bf16[3,128,512]{1,2,0:T(8,128)(2,1)S(1)}, bf16[3,128,512]{1,2,0:T(8,128)(2,1)}, u32[]{:S(2)}, u32[]{:S(2)}) collective-permute-start(bf16[3,128,512]{1,2,0:T(8,128)(2,1)S(1)} %copy.132), channel_id=1, source_target_pairs={{1,0},{2,1},{3,2},{4,3},{5,4},{6,5},{7,6},{0,7},{9,8},{10,9},{11,1... | collective-permute-start | bytes 1179656 | tf_op jit(solution)/shard_map/while/body/eval_jaxpr/ppermute | solution.py:16
  145.8 18.1 %collective-permute-start.1 = (bf16[3,128,512]{1,2,0:T(8,128)(2,1)S(1)}, bf16[3,128,512]{1,2,0:T(8,128)(2,1)}, u32[]{:S(2)}, u32[]{:S(2)}) collective-permute-start(bf16[3,128,512]{1,2,0:T(8,128)(2,1)S(1)} %copy.133), channel_id=1, source_target_pairs={{1,0},{2,1},{3,2},{4,3},{5,4},{6,5},{7,6},{0,7},{9,8},{10,9},{11,1... | collective-permute-start | bytes 1179656 | tf_op jit(solution)/shard_map/while/body/eval_jaxpr/ppermute | solution.py:16
  148.9 9.8 %collective-permute-start.2 = (bf16[3,128,512]{1,2,0:T(8,128)(2,1)}, bf16[3,128,512]{1,2,0:T(8,128)(2,1)}, u32[]{:S(2)}, u32[]{:S(2)}) collective-permute-start(bf16[3,128,512]{1,2,0:T(8,128)(2,1)} %fusion.113), channel_id=1, source_target_pairs={{1,0},{2,1},{3,2},{4,3},{5,4},{6,5},{7,6},{0,7},{9,8},{10,9},{11,1... | collective-permute-start | bytes 1179656 | tf_op jit(solution)/shard_map/while/body/eval_jaxpr/ppermute | solution.py:16
  150.1 12.8 %collective-permute-start.3 = (bf16[3,128,512]{1,2,0:T(8,128)(2,1)}, bf16[3,128,512]{1,2,0:T(8,128)(2,1)}, u32[]{:S(2)}, u32[]{:S(2)}) collective-permute-start(bf16[3,128,512]{1,2,0:T(8,128)(2,1)} %fusion.115), channel_id=1, source_target_pairs={{1,0},{2,1},{3,2},{4,3},{5,4},{6,5},{7,6},{0,7},{9,8},{10,9},{11,1... | collective-permute-start | bytes 1179656 | tf_op jit(solution)/shard_map/while/body/eval_jaxpr/ppermute | solution.py:16
  164.9 22.8 %collective-permute-start = (bf16[3,128,512]{1,2,0:T(8,128)(2,1)S(1)}, bf16[3,128,512]{1,2,0:T(8,128)(2,1)}, u32[]{:S(2)}, u32[]{:S(2)}) collective-permute-start(bf16[3,128,512]{1,2,0:T(8,128)(2,1)S(1)} %copy.132), channel_id=1, source_target_pairs={{1,0},{2,1},{3,2},{4,3},{5,4},{6,5},{7,6},{0,7},{9,8},{10,9},{11,1... | collective-permute-start | bytes 1179656 | tf_op jit(solution)/shard_map/while/body/eval_jaxpr/ppermute | solution.py:16
  169.6 18.1 %collective-permute-start.1 = (bf16[3,128,512]{1,2,0:T(8,128)(2,1)S(1)}, bf16[3,128,512]{1,2,0:T(8,128)(2,1)}, u32[]{:S(2)}, u32[]{:S(2)}) collective-permute-start(bf16[3,128,512]{1,2,0:T(8,128)(2,1)S(1)} %copy.133), channel_id=1, source_target_pairs={{1,0},{2,1},{3,2},{4,3},{5,4},{6,5},{7,6},{0,7},{9,8},{10,9},{11,1... | collective-permute-start | bytes 1179656 | tf_op jit(solution)/shard_map/while/body/eval_jaxpr/ppermute | solution.py:16
  172.7 9.8 %collective-permute-start.2 = (bf16[3,128,512]{1,2,0:T(8,128)(2,1)}, bf16[3,128,512]{1,2,0:T(8,128)(2,1)}, u32[]{:S(2)}, u32[]{:S(2)}) collective-permute-start(bf16[3,128,512]{1,2,0:T(8,128)(2,1)} %fusion.113), channel_id=1, source_target_pairs={{1,0},{2,1},{3,2},{4,3},{5,4},{6,5},{7,6},{0,7},{9,8},{10,9},{11,1... | collective-permute-start | bytes 1179656 | tf_op jit(solution)/shard_map/while/body/eval_jaxpr/ppermute | solution.py:16
  173.9 12.8 %collective-permute-start.3 = (bf16[3,128,512]{1,2,0:T(8,128)(2,1)}, bf16[3,128,512]{1,2,0:T(8,128)(2,1)}, u32[]{:S(2)}, u32[]{:S(2)}) collective-permute-start(bf16[3,128,512]{1,2,0:T(8,128)(2,1)} %fusion.115), channel_id=1, source_target_pairs={{1,0},{2,1},{3,2},{4,3},{5,4},{6,5},{7,6},{0,7},{9,8},{10,9},{11,1... | collective-permute-start | bytes 1179656 | tf_op jit(solution)/shard_map/while/body/eval_jaxpr/ppermute | solution.py:16
  188.8 22.8 %collective-permute-start = (bf16[3,128,512]{1,2,0:T(8,128)(2,1)S(1)}, bf16[3,128,512]{1,2,0:T(8,128)(2,1)}, u32[]{:S(2)}, u32[]{:S(2)}) collective-permute-start(bf16[3,128,512]{1,2,0:T(8,128)(2,1)S(1)} %copy.132), channel_id=1, source_target_pairs={{1,0},{2,1},{3,2},{4,3},{5,4},{6,5},{7,6},{0,7},{9,8},{10,9},{11,1... | collective-permute-start | bytes 1179656 | tf_op jit(solution)/shard_map/while/body/eval_jaxpr/ppermute | solution.py:16
  193.5 18.1 %collective-permute-start.1 = (bf16[3,128,512]{1,2,0:T(8,128)(2,1)S(1)}, bf16[3,128,512]{1,2,0:T(8,128)(2,1)}, u32[]{:S(2)}, u32[]{:S(2)}) collective-permute-start(bf16[3,128,512]{1,2,0:T(8,128)(2,1)S(1)} %copy.133), channel_id=1, source_target_pairs={{1,0},{2,1},{3,2},{4,3},{5,4},{6,5},{7,6},{0,7},{9,8},{10,9},{11,1... | collective-permute-start | bytes 1179656 | tf_op jit(solution)/shard_map/while/body/eval_jaxpr/ppermute | solution.py:16
  196.5 9.8 %collective-permute-start.2 = (bf16[3,128,512]{1,2,0:T(8,128)(2,1)}, bf16[3,128,512]{1,2,0:T(8,128)(2,1)}, u32[]{:S(2)}, u32[]{:S(2)}) collective-permute-start(bf16[3,128,512]{1,2,0:T(8,128)(2,1)} %fusion.113), channel_id=1, source_target_pairs={{1,0},{2,1},{3,2},{4,3},{5,4},{6,5},{7,6},{0,7},{9,8},{10,9},{11,1... | collective-permute-start | bytes 1179656 | tf_op jit(solution)/shard_map/while/body/eval_jaxpr/ppermute | solution.py:16
  197.7 12.8 %collective-permute-start.3 = (bf16[3,128,512]{1,2,0:T(8,128)(2,1)}, bf16[3,128,512]{1,2,0:T(8,128)(2,1)}, u32[]{:S(2)}, u32[]{:S(2)}) collective-permute-start(bf16[3,128,512]{1,2,0:T(8,128)(2,1)} %fusion.115), channel_id=1, source_target_pairs={{1,0},{2,1},{3,2},{4,3},{5,4},{6,5},{7,6},{0,7},{9,8},{10,9},{11,1... | collective-permute-start | bytes 1179656 | tf_op jit(solution)/shard_map/while/body/eval_jaxpr/ppermute | solution.py:16
  212.6 22.8 %collective-permute-start = (bf16[3,128,512]{1,2,0:T(8,128)(2,1)S(1)}, bf16[3,128,512]{1,2,0:T(8,128)(2,1)}, u32[]{:S(2)}, u32[]{:S(2)}) collective-permute-start(bf16[3,128,512]{1,2,0:T(8,128)(2,1)S(1)} %copy.132), channel_id=1, source_target_pairs={{1,0},{2,1},{3,2},{4,3},{5,4},{6,5},{7,6},{0,7},{9,8},{10,9},{11,1... | collective-permute-start | bytes 1179656 | tf_op jit(solution)/shard_map/while/body/eval_jaxpr/ppermute | solution.py:16
  217.3 18.1 %collective-permute-start.1 = (bf16[3,128,512]{1,2,0:T(8,128)(2,1)S(1)}, bf16[3,128,512]{1,2,0:T(8,128)(2,1)}, u32[]{:S(2)}, u32[]{:S(2)}) collective-permute-start(bf16[3,128,512]{1,2,0:T(8,128)(2,1)S(1)} %copy.133), channel_id=1, source_target_pairs={{1,0},{2,1},{3,2},{4,3},{5,4},{6,5},{7,6},{0,7},{9,8},{10,9},{11,1... | collective-permute-start | bytes 1179656 | tf_op jit(solution)/shard_map/while/body/eval_jaxpr/ppermute | solution.py:16
  220.4 9.8 %collective-permute-start.2 = (bf16[3,128,512]{1,2,0:T(8,128)(2,1)}, bf16[3,128,512]{1,2,0:T(8,128)(2,1)}, u32[]{:S(2)}, u32[]{:S(2)}) collective-permute-start(bf16[3,128,512]{1,2,0:T(8,128)(2,1)} %fusion.113), channel_id=1, source_target_pairs={{1,0},{2,1},{3,2},{4,3},{5,4},{6,5},{7,6},{0,7},{9,8},{10,9},{11,1... | collective-permute-start | bytes 1179656 | tf_op jit(solution)/shard_map/while/body/eval_jaxpr/ppermute | solution.py:16
  221.6 12.8 %collective-permute-start.3 = (bf16[3,128,512]{1,2,0:T(8,128)(2,1)}, bf16[3,128,512]{1,2,0:T(8,128)(2,1)}, u32[]{:S(2)}, u32[]{:S(2)}) collective-permute-start(bf16[3,128,512]{1,2,0:T(8,128)(2,1)} %fusion.115), channel_id=1, source_target_pairs={{1,0},{2,1},{3,2},{4,3},{5,4},{6,5},{7,6},{0,7},{9,8},{10,9},{11,1... | collective-permute-start | bytes 1179656 | tf_op jit(solution)/shard_map/while/body/eval_jaxpr/ppermute | solution.py:16
  236.4 22.8 %collective-permute-start = (bf16[3,128,512]{1,2,0:T(8,128)(2,1)S(1)}, bf16[3,128,512]{1,2,0:T(8,128)(2,1)}, u32[]{:S(2)}, u32[]{:S(2)}) collective-permute-start(bf16[3,128,512]{1,2,0:T(8,128)(2,1)S(1)} %copy.132), channel_id=1, source_target_pairs={{1,0},{2,1},{3,2},{4,3},{5,4},{6,5},{7,6},{0,7},{9,8},{10,9},{11,1... | collective-permute-start | bytes 1179656 | tf_op jit(solution)/shard_map/while/body/eval_jaxpr/ppermute | solution.py:16
  241.1 18.1 %collective-permute-start.1 = (bf16[3,128,512]{1,2,0:T(8,128)(2,1)S(1)}, bf16[3,128,512]{1,2,0:T(8,128)(2,1)}, u32[]{:S(2)}, u32[]{:S(2)}) collective-permute-start(bf16[3,128,512]{1,2,0:T(8,128)(2,1)S(1)} %copy.133), channel_id=1, source_target_pairs={{1,0},{2,1},{3,2},{4,3},{5,4},{6,5},{7,6},{0,7},{9,8},{10,9},{11,1... | collective-permute-start | bytes 1179656 | tf_op jit(solution)/shard_map/while/body/eval_jaxpr/ppermute | solution.py:16
  244.2 9.8 %collective-permute-start.2 = (bf16[3,128,512]{1,2,0:T(8,128)(2,1)}, bf16[3,128,512]{1,2,0:T(8,128)(2,1)}, u32[]{:S(2)}, u32[]{:S(2)}) collective-permute-start(bf16[3,128,512]{1,2,0:T(8,128)(2,1)} %fusion.113), channel_id=1, source_target_pairs={{1,0},{2,1},{3,2},{4,3},{5,4},{6,5},{7,6},{0,7},{9,8},{10,9},{11,1... | collective-permute-start | bytes 1179656 | tf_op jit(solution)/shard_map/while/body/eval_jaxpr/ppermute | solution.py:16
  245.4 12.8 %collective-permute-start.3 = (bf16[3,128,512]{1,2,0:T(8,128)(2,1)}, bf16[3,128,512]{1,2,0:T(8,128)(2,1)}, u32[]{:S(2)}, u32[]{:S(2)}) collective-permute-start(bf16[3,128,512]{1,2,0:T(8,128)(2,1)} %fusion.115), channel_id=1, source_target_pairs={{1,0},{2,1},{3,2},{4,3},{5,4},{6,5},{7,6},{0,7},{9,8},{10,9},{11,1... | collective-permute-start | bytes 1179656 | tf_op jit(solution)/shard_map/while/body/eval_jaxpr/ppermute | solution.py:16
  260.3 22.8 %collective-permute-start = (bf16[3,128,512]{1,2,0:T(8,128)(2,1)S(1)}, bf16[3,128,512]{1,2,0:T(8,128)(2,1)}, u32[]{:S(2)}, u32[]{:S(2)}) collective-permute-start(bf16[3,128,512]{1,2,0:T(8,128)(2,1)S(1)} %copy.132), channel_id=1, source_target_pairs={{1,0},{2,1},{3,2},{4,3},{5,4},{6,5},{7,6},{0,7},{9,8},{10,9},{11,1... | collective-permute-start | bytes 1179656 | tf_op jit(solution)/shard_map/while/body/eval_jaxpr/ppermute | solution.py:16
  265.0 18.1 %collective-permute-start.1 = (bf16[3,128,512]{1,2,0:T(8,128)(2,1)S(1)}, bf16[3,128,512]{1,2,0:T(8,128)(2,1)}, u32[]{:S(2)}, u32[]{:S(2)}) collective-permute-start(bf16[3,128,512]{1,2,0:T(8,128)(2,1)S(1)} %copy.133), channel_id=1, source_target_pairs={{1,0},{2,1},{3,2},{4,3},{5,4},{6,5},{7,6},{0,7},{9,8},{10,9},{11,1... | collective-permute-start | bytes 1179656 | tf_op jit(solution)/shard_map/while/body/eval_jaxpr/ppermute | solution.py:16
  268.0 9.8 %collective-permute-start.2 = (bf16[3,128,512]{1,2,0:T(8,128)(2,1)}, bf16[3,128,512]{1,2,0:T(8,128)(2,1)}, u32[]{:S(2)}, u32[]{:S(2)}) collective-permute-start(bf16[3,128,512]{1,2,0:T(8,128)(2,1)} %fusion.113), channel_id=1, source_target_pairs={{1,0},{2,1},{3,2},{4,3},{5,4},{6,5},{7,6},{0,7},{9,8},{10,9},{11,1... | collective-permute-start | bytes 1179656 | tf_op jit(solution)/shard_map/while/body/eval_jaxpr/ppermute | solution.py:16
  269.2 12.8 %collective-permute-start.3 = (bf16[3,128,512]{1,2,0:T(8,128)(2,1)}, bf16[3,128,512]{1,2,0:T(8,128)(2,1)}, u32[]{:S(2)}, u32[]{:S(2)}) collective-permute-start(bf16[3,128,512]{1,2,0:T(8,128)(2,1)} %fusion.115), channel_id=1, source_target_pairs={{1,0},{2,1},{3,2},{4,3},{5,4},{6,5},{7,6},{0,7},{9,8},{10,9},{11,1... | collective-permute-start | bytes 1179656 | tf_op jit(solution)/shard_map/while/body/eval_jaxpr/ppermute | solution.py:16
  309.7 9.3 %collective-permute-start.4 = (bf16[3,128,512]{2,1,0:T(8,128)(2,1)S(1)}, bf16[3,128,512]{2,1,0:T(8,128)(2,1)S(1)}, u32[]{:S(2)}, u32[]{:S(2)}) collective-permute-start(bf16[3,128,512]{2,1,0:T(8,128)(2,1)S(1)} %add_convert_fusion.3), channel_id=1, source_target_pairs={{1,0},{2,1},{3,2},{4,3},{5,4},{6,5},{7,6},{0,7},{9,8},{10,9},{11,1... | collective-permute-start | bytes 1179656 | tf_op jit(solution)/shard_map/ppermute | solution.py:16
  (56 other events, 388.1 us)
Sparse Core Ops, SparseCore 0:
  13.4 40.9 all-gather.4
  56.6 37.1 all-gather.2
  325.6 238.8 all-reduce.3
where the time goes:
time: 586 us; the launch traced here: 584 us
  waiting for transfers between devices  297 us (51%)
  matrix products  80 us (14%)
  other arithmetic  65.1 us (11%)
  local copies, waits for them, and re-layouts  56.5 us (10%)
  blocking collectives  41 us (7%)
  starting transfers between devices  29.4 us (5%)
  between operations  14.3 us (2%)
    psum x1, waiting for transfers between devices, body(): lax.psum((grad_query, grad_key, grad_value, grad_out_proj, grad_up, grad_...  188 us
    ppermute x30, waiting for transfers between devices, passed_along(): return lax.ppermute(block, axis, route)  59.2 us
    psum x1, blocking collectives, body(): lax.psum((grad_query, grad_key, grad_value, grad_out_proj, grad_up, grad_...  41 us
    ppermute x30, starting transfers between devices, passed_along(): return lax.ppermute(block, axis, route)  29.3 us
    all_gather x1, waiting for transfers between devices, body(): value_piece = lax.all_gather(value_low, 'seq', axis=1, tiled=True)  25.8 us
    all_gather x1, waiting for transfers between devices, body(): key_piece = lax.all_gather(key_low, 'seq', axis=1, tiled=True)  24.1 us
    unnamed x105, local copies, waits for them, and re-layouts  21.1 us
    while x28, local copies, waits for them, and re-layouts  14.3 us
  transfers between devices with their start and end apart: 33, of which 19 were waited for; matrix products, arithmetic and copies ran while one was open for 21% of the time, Pallas kernels for 0%

commit v1 on v0

v1 whole, which is shorter than its diff:
```python
import functools

import jax
import jax.numpy as jnp
from jax import lax
from jax.experimental import pallas as pl
from jax.experimental.pallas import tpu as pltpu
from jax.sharding import PartitionSpec as P

HEADS = 8
EPSILON = 1e-06
MASKED = -1e30
VMEM_LIMIT = 56 * 1024 * 1024
PIECES = 16
BF16 = jnp.bfloat16
F32 = jnp.float32
GELU_C = 0.7978845608028654
GELU_A = 0.044715


def nn(a, b):
    return jnp.dot(a, b, preferred_element_type=F32)


def nt(a, b):
    return lax.dot_general(a, b, (((1,), (1,)), ((), ())), preferred_element_type=F32)


def tn(a, b):
    return lax.dot_general(a, b, (((0,), (0,)), ((), ())), preferred_element_type=F32)


def normalize(values):
    center = values - jnp.mean(values, axis=-1, keepdims=True)
    scale = lax.rsqrt(jnp.mean(center * center, axis=-1, keepdims=True) + EPSILON)
    return center * scale, scale


def norm_back(cotangent, unit, scale, gain):
    g = cotangent * gain
    return scale * (
        g
        - jnp.mean(g, axis=-1, keepdims=True)
        - unit * jnp.mean(g * unit, axis=-1, keepdims=True)
    )


def segments(pos, sp, layout, row):
    seg = jnp.zeros(pos.shape, jnp.int32)
    for j in range(layout.segs):
        seg += (pos >= sp[layout.offsets + row * layout.segs + j]).astype(jnp.int32)
    return seg + layout.segs * (pos >= sp[layout.crop + row]).astype(jnp.int32)


class Layout:
    def __init__(self, stations, rows, segs):
        self.core, self.other, self.ids = 0, 1, 2
        self.station = 5
        self.offsets = self.station + stations
        self.crop = self.offsets + rows * segs
        self.segs = segs


def positions(sp, layout, chunk, tok, shape, dim):
    start = sp[layout.station + chunk] * (2 * tok)
    i = lax.broadcasted_iota(jnp.int32, shape, dim)
    mine = start + sp[layout.core] * tok
    other = start + sp[layout.other] * tok - tok
    return i + jnp.where(i < tok, mine, other)


def chunk_kernel(layout, chunk, first, last, tok, rows, *refs):
    refs = list(refs)
    sp = refs.pop(0)
    xm, xo, gain, shift, wk, wv, bv = refs[:7]
    refs = refs[7:]
    if first:
        wq, bq = refs[:2]
        refs = refs[2:]
    else:
        qm_in, m_in, l_in, acc_in = refs[:4]
        refs = refs[4:]
    k_out, v_out, kt_out, nt_out, unit_out = refs[:5]
    refs = refs[5:]
    if first:
        qm_out = refs.pop(0)
    if last:
        lse_out, ot_out, att_m, att_o = refs[:4]
        refs = refs[4:]
        m_ref, l_ref, acc_ref = refs
    else:
        m_out, l_out, acc_out = refs
    half = wk.shape[1]
    heads = HEADS // 2
    size = half // heads
    chip = 2 * tok
    for at, x in ((0, xm), (tok, xo)):
        values = x[...].reshape(rows * tok, -1).astype(F32)
        unit, _ = normalize(values)
        normed = (unit * gain[...] + shift[...]).astype(BF16)
        k = nn(normed, wk[...]).astype(BF16)
        v = (nn(normed, wv[...]) + bv[...]).astype(BF16)
        if first:
            q = ((nn(normed, wq[...]) + bq[...]).astype(BF16).astype(F32) * size**-0.5).astype(BF16)
            lane = lax.broadcasted_iota(jnp.int32, (tok, 2 * size), 1)
        for r in range(rows):
            part = slice(r * tok, (r + 1) * tok)
            k_out[0, r, at : at + tok, :] = k[part]
            v_out[0, r, at : at + tok, :] = v[part]
            kt_out[0, r, :, at : at + tok] = k[part].astype(F32).T.astype(BF16)
            nt_out[0, r, :, at : at + tok] = normed[part].astype(F32).T.astype(BF16)
            unit_out[0, r, at : at + tok, :] = unit[part].astype(BF16)
            if first:
                for h in range(heads):
                    pair = q[part, (h // 2) * 2 * size : (h // 2 + 1) * 2 * size]
                    keep = (lane >= size) if h % 2 else (lane < size)
                    qm_out[r * heads + h, at : at + tok, :] = jnp.where(keep, pair, jnp.zeros_like(pair))
    qm = qm_out if first else qm_in
    for r in range(rows):
        key_seg = segments(positions(sp, layout, chunk, tok, (chip, chip), 0), sp, layout, r)
        query_seg = segments(positions(sp, layout, 0, tok, (1, chip), 1), sp, layout, r)
        bias = jnp.where(key_seg == query_seg, 0.0, MASKED)
        for h in range(heads):
            lanes = slice((h // 2) * 2 * size, (h // 2 + 1) * 2 * size)
            at = r * heads + h
            s = nt(k_out[0, r, :, lanes], qm[at]) + bias
            top = jnp.max(s, axis=0, keepdims=True)
            if not first:
                old = m_in[at]
                top = jnp.maximum(old, top)
            p = jnp.exp(s - top)
            total = jnp.sum(p, axis=0, keepdims=True)
            added = tn(v_out[0, r, :, lanes], p.astype(BF16))
            added = added[(h % 2) * size : (h % 2 + 1) * size]
            if not first:
                keep = jnp.exp(old - top)
                total += l_in[at] * keep
                added += acc_in[at] * keep
            if last:
                m_ref[at] = top
                l_ref[at] = total
                acc_ref[at] = added
            else:
                m_out[at] = top
                l_out[at] = total
                acc_out[at] = added
        if last:
            parts = []
            for h in range(heads):
                at = r * heads + h
                lse_out[at] = m_ref[at] + jnp.log(l_ref[at])
                out = acc_ref[at] / l_ref[at]
                ot_out[at] = out
                parts.append(out)
            att = jnp.concatenate(parts, axis=0).T.astype(BF16)
            att_m[r] = att[:tok]
            att_o[r] = att[tok:]


def ffn_kernel(
    sp, att_m, att_o, wo_m, wo_o, tokens, cot, up_m, up_o, down_m, down_o, b_out, bup_m, bup_o,
    b_down, gain, shift, out, hid_m, hid_o, pre_m, pre_o, normed_out, mid_grad, branch, vec
):
    rows, tok, width = tokens.shape
    flat = rows * tok
    x = tokens[...].reshape(flat, width).astype(F32)
    mid = (
        x
        + nn(att_m[...].reshape(flat, -1), wo_m[...])
        + nn(att_o[...].reshape(flat, -1), wo_o[...])
        + b_out[...]
    )
    unit, scale = normalize(mid)
    normed = (unit * gain[...] + shift[...]).astype(BF16)
    normed_out[...] = normed
    g = cot[...].reshape(flat, width)
    total = jnp.zeros((flat, width), F32)
    back = jnp.zeros((flat, width), F32)
    block = 512
    for which, (up, down, bup, hid, pre) in enumerate(
        ((up_m, down_m, bup_m, hid_m, pre_m), (up_o, down_o, bup_o, hid_o, pre_o))
    ):
        for j in range(up.shape[1] // block):
            cols = slice(j * block, (j + 1) * block)
            u = nn(normed, up[:, cols]) + bup[:, cols]
            square = u * u
            t = jnp.tanh(GELU_C * u * (1.0 + GELU_A * square))
            hidden = (0.5 * u * (1.0 + t)).astype(BF16)
            slope = 0.5 * (1.0 + t) + 0.5 * GELU_C * u * (1.0 - t * t) * (1.0 + 3 * GELU_A * square)
            pg = (nt(g, down[cols, :]) * slope).astype(BF16)
            hid[:, cols] = hidden
            pre[:, cols] = pg
            total += nn(hidden, down[cols, :])
            back += nt(pg, up[:, cols])
            n = up.shape[1] // block
            base = sp[1 if which else 0] * n
            vec[pl.ds(base + j, 1), :] = jnp.sum(pg.astype(F32), axis=0, keepdims=True)
    out[...] = (mid + total + b_down[...]).astype(BF16).reshape(rows, tok, width)
    gf = g.astype(F32)
    grad = gf + norm_back(back, unit, scale, gain[...])
    mid_grad[...] = grad
    low = grad.astype(BF16)
    branch[...] = low.reshape(rows, tok, width)
    vec[4:5, :] = jnp.sum(gf, axis=0, keepdims=True)
    vec[5:6, :] = jnp.sum(back * unit, axis=0, keepdims=True)
    vec[6:7, :] = jnp.sum(back, axis=0, keepdims=True)
    vec[7:8, :] = jnp.sum(low.astype(F32), axis=0, keepdims=True)


def ffn_grad_kernel(sp, hid_m, hid_r, g_m, g_o, n_m, n_o, pre_m, pre_r, down, up):
    gd = tn(hid_m[...], g_m[...]) + tn(hid_r[...], g_o[...])
    gu = tn(n_m[...], pre_m[...]) + tn(n_o[...], pre_r[...])
    rd = gd.shape[0] // PIECES
    ru = gu.shape[0] // PIECES
    for p in range(PIECES):
        down[p ^ sp[2]] = gd[p * rd : (p + 1) * rd].astype(BF16)
        up[p ^ sp[3]] = gu[p * ru : (p + 1) * ru].astype(BF16)


def attend_back_kernel(
    layout, tok, rows, sp, br_m, br_o, wo, qm, lse, ot, wq, wk, wv, vec_in, k, v, kt, norm_t, unit,
    dn_m, dn_o, pieces, do, dm, delta, dqt, gk, gv, vec
):
    step = pl.program_id(0)
    steps = pl.num_programs(0)
    heads = HEADS // 2
    half = wq.shape[1]
    size = half // heads
    chip = 2 * tok
    width = wq.shape[0]
    chunk = lax.rem(step + 1, steps)

    @pl.when(step == 0)
    def _():
        dqt[...] = jnp.zeros_like(dqt)
        gk[...] = jnp.zeros_like(gk)
        gv[...] = jnp.zeros_like(gv)
        vec[...] = jnp.zeros_like(vec)
        lane = lax.broadcasted_iota(jnp.int32, (tok, 2 * size), 1)
        for r in range(rows):
            for at, br in ((0, br_m), (tok, br_o)):
                low = nt(br[r], wo[...]).astype(BF16)
                do[r, at : at + tok, :] = low
                for h in range(heads):
                    pair = low[:, (h // 2) * 2 * size : (h // 2 + 1) * 2 * size]
                    keep = (lane >= size) if h % 2 else (lane < size)
                    dm[r * heads + h, at : at + tok, :] = jnp.where(keep, pair, jnp.zeros_like(pair))
            dot = do[r].astype(F32).T
            for h in range(heads):
                at = r * heads + h
                delta[at] = jnp.sum(ot[at] * dot[h * size : (h + 1) * size], axis=0, keepdims=True)

    for r in range(rows):
        key_seg = segments(positions(sp, layout, chunk, tok, (chip, chip), 0), sp, layout, r)
        query_seg = segments(positions(sp, layout, 0, tok, (1, chip), 1), sp, layout, r)
        bias = jnp.where(key_seg == query_seg, 0.0, MASKED)
        dks, dvs = [], []
        for pair in range(heads // 2):
            lanes = slice(pair * 2 * size, (pair + 1) * 2 * size)
            dk = dv = None
            for h in (2 * pair, 2 * pair + 1):
                at = r * heads + h
                p = jnp.exp(nt(k[0, r, :, lanes], qm[at]) + bias - lse[at])
                dp = nt(v[0, r, :, lanes], dm[at])
                ds = (p * (dp - delta[at])).astype(BF16)
                p = p.astype(BF16)
                dv_h, dk_h = nn(p, dm[at]), nn(ds, qm[at])
                dv = dv_h if dv is None else dv + dv_h
                dk = dk_h if dk is None else dk + dk_h
                dqt[r, h * size : (h + 1) * size, :] += nn(kt[0, r, h * size : (h + 1) * size, :], ds)
            dks.append(dk.astype(BF16))
            dvs.append(dv.astype(BF16))
        dk = jnp.concatenate(dks, axis=1)
        dv = jnp.concatenate(dvs, axis=1)
        gk[...] += nn(norm_t[0, r], dk)
        gv[...] += nn(norm_t[0, r], dv)
        vec[1:2, :half] += jnp.sum(dv.astype(F32), axis=0, keepdims=True)
        dn = nt(dk, wk[...]) + nt(dv, wv[...])
        dn_m[0, r] = dn[:tok].astype(BF16)
        dn_o[0, r] = dn[tok:].astype(BF16)
        u = unit[0, r].astype(F32)
        vec[8:9, :] += jnp.sum(dn * u, axis=0, keepdims=True)
        vec[9:10, :] += jnp.sum(dn, axis=0, keepdims=True)

    @pl.when(step == steps - 1)
    def _():
        gq = jnp.zeros((width, half), F32)
        go = jnp.zeros((half, width), F32)
        for r in range(rows):
            dq = (dqt[r] * size**-0.5).T.astype(BF16)
            gq += nn(norm_t[0, r], dq)
            dn = nt(dq, wq[...])
            dn_m[0, r] = (dn_m[0, r].astype(F32) + dn[:tok]).astype(BF16)
            dn_o[0, r] = (dn_o[0, r].astype(F32) + dn[tok:]).astype(BF16)
            u = unit[0, r].astype(F32)
            vec[0:1, :half] += jnp.sum(dq.astype(F32), axis=0, keepdims=True)
            vec[8:9, :] += jnp.sum(dn * u, axis=0, keepdims=True)
            vec[9:10, :] += jnp.sum(dn, axis=0, keepdims=True)
            out_t = jnp.concatenate([ot[r * heads + h] for h in range(heads)], axis=0).astype(BF16)
            go += nn(out_t[:, :tok], br_m[r]) + nn(out_t[:, tok:], br_o[r])
        lane = lax.broadcasted_iota(jnp.int32, (2, width), 1)
        both = vec[0:2, :half]
        both = jnp.concatenate([both, both], axis=1)
        vec[0:2, :] = jnp.where((lane >= half) == (sp[layout.core] == 1), both, 0.0)
        vec[2:3, :] = vec_in[7:8, :]
        vec[3:4, :] = vec_in[4:5, :]
        vec[4:8, :] = vec_in[0:4, :]
        vec[10:12, :] = vec_in[5:7, :]
        n = width // PIECES
        low = n // 2
        for piece in range(PIECES):
            slot = piece ^ sp[4]
            part = slice(piece * n, (piece + 1) * n)
            pieces[slot, 0:n, :half] = gq[part].astype(BF16)
            pieces[slot, 0:n, half:] = gk[part].astype(BF16)
            pieces[slot, n : n + low, :half] = gv[part][:low].astype(BF16)
            pieces[slot, n : n + low, half:] = gv[part][low:].astype(BF16)
            pieces[slot, n + low : 2 * n, :] = go[piece * low : (piece + 1) * low].astype(BF16)
            row = vec[piece : piece + 1, :]
            pad = jnp.concatenate([row, jnp.zeros((15, width), F32)], axis=0)
            pieces[slot, 2 * n : 2 * n + 16, :] = pad.astype(BF16)


def last_kernel(tokens, gain, mid_grad, own, arrived, out):
    rows, tok, width = tokens.shape
    flat = rows * tok
    unit, scale = normalize(tokens[...].reshape(flat, width).astype(F32))
    dn = own[...].astype(F32) + arrived[...].astype(F32)
    grad = mid_grad[...] + norm_back(dn.reshape(flat, width), unit, scale, gain[...])
    out[...] = grad.astype(BF16).reshape(rows, tok, width)


def unpack_ffn_kernel(sp, d_m, d_o, u_m, u_o, down, up):
    rd, ru, cols = d_m.shape[1], u_m.shape[1], u_m.shape[2]
    for p in range(PIECES):
        for which, d, u in ((0, d_m, u_m), (1, d_o, u_o)):
            c = sp[which]
            down[pl.ds(c * (PIECES * rd) + p * rd, rd), :] = d[p ^ sp[2]].astype(F32)
            up[p * ru : (p + 1) * ru, pl.ds(pl.multiple_of(c * cols, 128), cols)] = u[p ^ sp[3]].astype(F32)


def unpack_attend_kernel(sp, a_m, a_o, gq, gk, gv, go, vec):
    width = gq.shape[0]
    half = width // 2
    n = width // PIECES
    low = n // 2
    for p in range(PIECES):
        row = jnp.zeros((1, width), F32)
        for which, a in ((0, a_m), (1, a_o)):
            c = sp[which]
            slot = p ^ sp[4]
            cols = pl.ds(pl.multiple_of(c * half, 128), half)
            gq[p * n : (p + 1) * n, cols] = a[slot, 0:n, :half].astype(F32)
            gk[p * n : (p + 1) * n, cols] = a[slot, 0:n, half:].astype(F32)
            gv[p * n : p * n + low, cols] = a[slot, n : n + low, :half].astype(F32)
            gv[p * n + low : (p + 1) * n, cols] = a[slot, n : n + low, half:].astype(F32)
            go[pl.ds(c * half + p * low, low), :] = a[slot, n + low : 2 * n, :].astype(F32)
            row += a[slot, 2 * n : 2 * n + 16, :].astype(F32)[0:1]
        vec[p : p + 1, :] = row


def whole(shape):
    zeros = (0,) * len(shape)
    return pl.BlockSpec(shape, lambda *_: zeros)


def half_cols(shape, which):
    return pl.BlockSpec((shape[0], shape[1] // 2), lambda i, sp: (0, sp[which]))


def half_rows(shape, which):
    return pl.BlockSpec((shape[0] // 2, shape[1]), lambda i, sp: (sp[which], 0))


def call(kernel, sp, ins, outs, scratch=(), grid=(1,), flops=0, moved=0, name=None):
    return pl.pallas_call(
        kernel,
        grid_spec=pltpu.PrefetchScalarGridSpec(
            num_scalar_prefetch=1,
            grid=grid,
            in_specs=[spec for _, spec in ins],
            out_specs=[spec for _, spec in outs],
            scratch_shapes=list(scratch),
        ),
        out_shape=[shape for shape, _ in outs],
        compiler_params=pltpu.CompilerParams(vmem_limit_bytes=VMEM_LIMIT),
        cost_estimate=pl.CostEstimate(flops=flops, bytes_accessed=moved, transcendentals=0),
        name=name,
    )(sp, *[a for a, _ in ins])


def full(array):
    return (array, whole(array.shape))


def made(shape, dtype):
    return (jax.ShapeDtypeStruct(shape, dtype), whole(shape))


def exchange(array, axis, mask):
    count = lax.axis_size(axis)
    return lax.ppermute(array, axis, [(i, i ^ mask) for i in range(count)])


def ring_order(count):
    return list(range(0, count, 2)) + list(range(1, count, 2))[::-1]


def added(*parts):
    return sum(p.astype(F32) for p in parts).astype(BF16)


def reduce_pieces(buf, bits, rest):
    for axis, mask in bits:
        half = buf.shape[0] // 2
        buf = added(buf[:half], exchange(buf[half:], axis, mask))
    for axis, mask in rest:
        buf = added(buf, exchange(buf, axis, mask))
    return buf


def spread_pieces(buf, bits):
    for axis, mask in reversed(bits):
        buf = jnp.concatenate([buf, exchange(buf, axis, mask)], axis=0)
    return buf


def my_id(bits):
    out = 0
    for axis, mask in bits:
        out = out * 2 + jnp.where((lax.axis_index(axis) & mask) != 0, 1, 0)
    return out


def body(
    tokens, grad_out, crop, offsets, w_query, w_key, w_value, w_out, w_up, w_down, b_query, b_value,
    b_out, b_up, b_down, gain_one, shift_one, gain_two, shift_two,
):
    rows, tok, width = tokens.shape
    seq_count, dp_count = lax.axis_size("seq"), lax.axis_size("dp")
    stations = seq_count // 2
    hidden = w_up.shape[1]
    half = width // 2
    heads = HEADS // 2
    chip = 2 * tok
    flat = rows * tok
    segs = offsets.shape[1]
    layout = Layout(stations, rows, segs)
    seq = lax.axis_index("seq")
    core, station = seq % 2, seq // 2

    order = ring_order(stations)
    place = {s: i for i, s in enumerate(order)}
    table = jnp.array(
        [[order[(place[s] - j) % stations] for j in range(stations)] for s in range(stations)], jnp.int32
    )
    ring = []
    for i, s in enumerate(order):
        after = order[(i + 1) % stations]
        ring += [(2 * s + c, 2 * after + c) for c in range(2)]

    dp_bits = [("dp", 1 << i) for i in range(dp_count.bit_length() - 1)]
    st_bits = [("seq", 2 << i) for i in range(stations.bit_length() - 1)]
    chosen = (dp_bits[:2] + st_bits[:2])[: PIECES.bit_length() - 1]
    rest = dp_bits[2:] + st_bits[2:]
    swapped = [chosen[1], chosen[0]] + chosen[2:]
    bits = (chosen, swapped, chosen)

    sp = jnp.concatenate(
        [
            jnp.stack([core, 1 - core] + [my_id(b) for b in bits]).astype(jnp.int32),
            lax.dynamic_slice(table, (station, 0), (1, stations))[0],
            offsets.reshape(-1),
            crop,
        ]
    )
    line = lambda v: v.reshape(1, -1)

    block = tokens
    k_parts, state = [], None
    keys, values, keys_t, norm_t, units = [], [], [], [], []
    for j in range(stations):
        if j:
            block = lax.ppermute(block, "seq", ring)
        other = exchange(block, "seq", 1)
        first, last = j == 0, j == stations - 1
        ins = [full(block), full(other), full(line(gain_one)), full(line(shift_one))]
        ins += [(w_key, half_cols(w_key.shape, 0)), (w_value, half_cols(w_value.shape, 0))]
        ins += [(line(b_value), half_cols((1, width), 0))]
        if first:
            ins += [(w_query, half_cols(w_query.shape, 0)), (line(b_query), half_cols((1, width), 0))]
        else:
            ins += [full(a) for a in state]
        outs = [
            made((1, rows, chip, half), BF16),
            made((1, rows, chip, half), BF16),
            made((1, rows, half, chip), BF16),
            made((1, rows, width, chip), BF16),
            made((1, rows, chip, width), BF16),
        ]
        if first:
            outs += [made((rows * heads, chip, 2 * half // heads), BF16)]
        stat = made((rows * heads, 1, chip), F32)
        acc = made((rows * heads, half // heads, chip), F32)
        scratch = []
        if last:
            outs += [stat, acc, made((rows, tok, half), BF16), made((rows, tok, half), BF16)]
            scratch = [pltpu.VMEM(s.shape, F32) for s in (stat[0], stat[0], acc[0])]
        else:
            outs += [stat, stat, acc]
        got = call(
            functools.partial(chunk_kernel, layout, j, first, last, tok, rows),
            sp, ins, outs, scratch, flops=6 * 10**8, moved=4 * 10**6, name=f"attend_chunk_{j}",
        )
        for where, array in zip((keys, values, keys_t, norm_t, units), got[:5]):
            where.append(array)
        got = got[5:]
        if first:
            query, got = got[0], got[1:]
        if not last:
            state = [query] + list(got)
    lse, out_t, att_m, att_o = got
    att_r = exchange(att_o, "seq", 1)
    g_other = exchange(grad_out, "seq", 1)

    res = call(
        ffn_kernel, sp,
        [
            full(att_m), full(att_r),
            (w_out, half_rows(w_out.shape, 0)), (w_out, half_rows(w_out.shape, 1)),
            full(tokens), full(grad_out),
            (w_up, half_cols(w_up.shape, 0)), (w_up, half_cols(w_up.shape, 1)),
            (w_down, half_rows(w_down.shape, 0)), (w_down, half_rows(w_down.shape, 1)),
            full(line(b_out)),
            (line(b_up), half_cols((1, hidden), 0)), (line(b_up), half_cols((1, hidden), 1)),
            full(line(b_down)), full(line(gain_two)), full(line(shift_two)),
        ],
        [made((rows, tok, width), BF16)]
        + [made((flat, hidden // 2), BF16)] * 4
        + [made((flat, width), BF16), made((flat, width), F32), made((rows, tok, width), BF16), made((8, width), F32)],
        flops=4 * 10**9, moved=10**7, name="feed_forward",
    )
    outputs, hid_m, hid_o, pre_m, pre_o, normed_two, mid_grad, branch, vec_ffn = res
    branch_r = exchange(branch, "seq", 1)
    hid_r = exchange(hid_o, "seq", 1)
    pre_r = exchange(pre_o, "seq", 1)
    normed_two_r = exchange(normed_two, "seq", 1)

    down, up = call(
        ffn_grad_kernel, sp,
        [
            full(hid_m), full(hid_r), full(grad_out.reshape(flat, width)), full(g_other.reshape(flat, width)),
            full(normed_two), full(normed_two_r), full(pre_m), full(pre_r),
        ],
        [
            made((PIECES, hidden // 2 // PIECES, width), BF16),
            made((PIECES, width // PIECES, hidden // 2), BF16),
        ],
        flops=16 * 10**8, moved=5 * 10**6, name="feed_forward_grad",
    )

    joined = lambda parts: jnp.concatenate(parts, axis=0)
    k_all, v_all, kt_all, nt_all, unit_all = map(joined, (keys, values, keys_t, norm_t, units))

    def per_chunk(array):
        shape = (1,) + array.shape[1:]
        return (array, pl.BlockSpec(shape, lambda i, sp: (lax.rem(i + 1, stations), 0, 0, 0)))

    dn_shape = jax.ShapeDtypeStruct((stations, rows, tok, width), BF16)
    dn_m, dn_o, pieces = call(
        functools.partial(attend_back_kernel, layout, tok, rows), sp,
        [
            full(branch), full(branch_r), (w_out, half_rows(w_out.shape, 0)), full(query), full(lse), full(out_t),
            (w_query, half_cols(w_query.shape, 0)), (w_key, half_cols(w_key.shape, 0)),
            (w_value, half_cols(w_value.shape, 0)), full(vec_ffn),
        ]
        + [per_chunk(a) for a in (k_all, v_all, kt_all, nt_all, unit_all)],
        [per_chunk(dn_shape), per_chunk(dn_shape), made((PIECES, 2 * width // PIECES + 16, width), BF16)],
        scratch=[
            pltpu.VMEM((rows, chip, half), BF16),
            pltpu.VMEM((rows * heads, chip, 2 * half // heads), BF16),
            pltpu.VMEM((rows * heads, 1, chip), F32),
            pltpu.VMEM((rows, half, chip), F32),
            pltpu.VMEM((width, half), F32),
            pltpu.VMEM((width, half), F32),
            pltpu.VMEM((16, width), F32),
        ],
        grid=(stations,), flops=8 * 10**9, moved=10**7, name="attend_back",
    )

    arrived = None
    for j in range(1, stations):
        part = [dn_m[j], exchange(dn_o[j], "seq", 1)]
        if arrived is not None:
            part.append(arrived)
        arrived = lax.ppermute(added(*part), "seq", ring)
    own = added(dn_m[0], exchange(dn_o[0], "seq", 1))

    def reduced(buf, which):
        buf = spread_pieces(reduce_pieces(buf, bits[which], rest), bits[which])
        return buf, exchange(buf, "seq", 1)

    down_m, down_o = reduced(down, 0)
    up_m, up_o = reduced(up, 1)
    att_pieces, att_other = reduced(pieces, 2)

    if arrived is None:
        arrived = jnp.zeros_like(own)
    input_grad = pl.pallas_call(
        last_kernel,
        out_shape=jax.ShapeDtypeStruct((rows, tok, width), BF16),
        compiler_params=pltpu.CompilerParams(vmem_limit_bytes=VMEM_LIMIT),
        name="input_grad",
    )(tokens, line(gain_one), mid_grad, own, arrived)

    grad_down, grad_up = call(
        unpack_ffn_kernel, sp,
        [full(down_m), full(down_o), full(up_m), full(up_o)],
        [made((hidden, width), F32), made((width, hidden), F32)],
        name="unpack_feed_forward",
    )
    square = made((width, width), F32)
    grad_query, grad_key, grad_value, grad_out_proj, vec = call(
        unpack_attend_kernel, sp,
        [full(att_pieces), full(att_other)],
        [square, square, square, square, made((PIECES, width), F32)],
        name="unpack_attend",
    )
    return (
        outputs, input_grad, grad_query, grad_key, grad_value, grad_out_proj, grad_up, grad_down,
        vec[0], vec[1], vec[2], vec[4:8].reshape(-1), vec[3], vec[8], vec[9], vec[10], vec[11],
    )


def solution(mesh):
    split, row, copied = P("dp", "seq", None), P("dp"), P()
    return jax.shard_map(
        body,
        mesh=mesh,
        in_specs=(split, split, row, P("dp", None)) + (copied,) * 15,
        out_specs=(split, split) + (copied,) * 15,
        check_vma=False,
    )
```

time: 586 us -> 269 us (0.46)
  waiting for transfers between devices: 297 us -> 95 us
  Pallas kernels: 0 us -> 89.8 us
  matrix products: 80 us -> 0 us
  other arithmetic: 65.1 us -> 11.7 us
  blocking collectives: 41 us -> 0 us
  local copies, waits for them, and re-layouts: 56.5 us -> 18 us
  starting transfers between devices: 29.4 us -> 52.1 us
  between operations: 14.3 us -> 1.34 us
    psum x1 -> x0, waiting for transfers between devices: 188 us -> none  [body(): lax.psum((grad_query, grad_key, grad_value, grad_out_proj, grad_up, grad_...]
    pallas_call x0 -> x10, Pallas kernels: none -> 89.8 us  [the longest x9 87 us: call(): pl.pallas_call(kernel, grid_spec=pltpu.PrefetchScalarGridSpec(num_scalar_...]
    dot_general x60 -> x0, matrix products: 80 us -> none  [the longest x9 11.3 us: block_scores(): jnp.einsum('rqhe,rkhe->rhqk', query_rows, key_rows, preferred_element_typ...]
    all_gather x2 -> x0, waiting for transfers between devices: 49.8 us -> none  [the longest x1 25.8 us: body(): value_piece = lax.all_gather(value_low, 'seq', axis=1, tiled=True)]
    psum x1 -> x0, blocking collectives: 41 us -> none  [body(): lax.psum((grad_query, grad_key, grad_value, grad_out_proj, grad_up, grad_...]
    ppermute x30 -> x47, waiting for transfers between devices: 59.2 us -> 95 us  [the longest x41 57.3 us: exchange(): return lax.ppermute(array, axis, [(i, i ^ mask) for i in range(count)])]
    convert_element_type x32 -> x12, other arithmetic: 38.3 us -> 3.2 us  [added(): return sum((p.astype(F32) for p in parts)).astype(BF16)]
    ppermute x30 -> x47, starting transfers between devices: 29.3 us -> 52.1 us  [the longest x41 37.3 us: exchange(): return lax.ppermute(array, axis, [(i, i ^ mask) for i in range(count)])]
  transfers between devices with their start and end apart: 33 -> 47, of which waited for: 19 -> 20; matrix products, arithmetic and copies ran while one was open for 21% -> 6% of each run, Pallas kernels for 0% -> 15%
where the time goes in v1:
time: 269 us; the launch traced here: 268 us
  waiting for transfers between devices  95 us (35%)
  Pallas kernels  89.8 us (33%)
  starting transfers between devices  52.1 us (19%)
  local copies, waits for them, and re-layouts  18 us (7%)
  other arithmetic  11.7 us (4%)
    pallas_call x9, Pallas kernels, call(): pl.pallas_call(kernel, grid_spec=pltpu.PrefetchScalarGridSpec(num_scalar_...  87 us
    ppermute x41, waiting for transfers between devices, exchange(): return lax.ppermute(array, axis, [(i, i ^ mask) for i in range(count)])  57.3 us
    ppermute x41, starting transfers between devices, exchange(): return lax.ppermute(array, axis, [(i, i ^ mask) for i in range(count)])  37.3 us
    ppermute x3, waiting for transfers between devices, body(): block = lax.ppermute(block, 'seq', ring)  22.3 us
    ppermute x3, waiting for transfers between devices, body(): arrived = lax.ppermute(added(*part), 'seq', ring)  15.4 us
    ppermute x3, starting transfers between devices, body(): block = lax.ppermute(block, 'seq', ring)  10.7 us
    unnamed x103, local copies, waits for them, and re-layouts  9.72 us
    concatenate x4, other arithmetic, body(): joined = lambda parts: jnp.concatenate(parts, axis=0)  8.15 us
  transfers between devices with their start and end apart: 47, of which 20 were waited for; matrix products, arithmetic and copies ran while one was open for 6% of the time, Pallas kernels for 15%

profile of v1, /device:TPU:0, one launch (start us, length us, event | category | flops | bytes accessed | tf_op | source)
XLA Modules:
  0.0 268.0 jit_solution(13234711781237791748)
XLA Ops:
  0.7 4.1 %collective-permute-start = (bf16[3,128,512]{2,1,0:T(8,128)(2,1)}, bf16[3,128,512]{2,1,0:T(8,128)(2,1)S(1)}, u32[]{:S(2)}, u32[]{:S(2)}) collective-permute-start(bf16[3,128,512]{2,1,0:T(8,128)(2,1)} %tokens.3), channel_id=1, source_target_pairs={{0,4},{1,5},{4,6},{5,7},{6,2},{7,3},{2,0},{3,1},{8,12},{9,13},{12,... | collective-permute-start | bytes 1179656 | tf_op jit(solution)/shard_map/ppermute | solution.py:484
  4.7 8.7 %collective-permute-done.refs_1_ = bf16[3,128,512]{2,1,0:T(8,128)(2,1)S(1)} collective-permute-done((bf16[3,128,512]{2,1,0:T(8,128)(2,1)}, bf16[3,128,512]{2,1,0:T(8,128)(2,1)S(1)}, u32[]{:S(2)}, u32[]{:S(2)}) %collective-permute-start) | collective-permute-done | bytes 393248 | tf_op jit(solution)/shard_map/ppermute | solution.py:484
  13.4 3.3 %collective-permute-start.1 = (bf16[3,128,512]{2,1,0:T(8,128)(2,1)S(1)}, bf16[3,128,512]{2,1,0:T(8,128)(2,1)S(1)}, u32[]{:S(2)}, u32[]{:S(2)}) collective-permute-start(bf16[3,128,512]{2,1,0:T(8,128)(2,1)S(1)} %collective-permute-done.refs_1_), channel_id=1, source_target_pairs={{0,4},{1,5},{4,6},{5,7},{6,2},{7,3},{2,0},{3,1},{8,12},{9,13},{12,... | collective-permute-start | bytes 1179656 | tf_op jit(solution)/shard_map/ppermute | solution.py:484
  16.7 7.5 %collective-permute-done.1.refs_1_ = bf16[3,128,512]{2,1,0:T(8,128)(2,1)S(1)} collective-permute-done((bf16[3,128,512]{2,1,0:T(8,128)(2,1)S(1)}, bf16[3,128,512]{2,1,0:T(8,128)(2,1)S(1)}, u32[]{:S(2)}, u32[]{:S(2)}) %collective-permute-start.1) | collective-permute-done | bytes 393248 | tf_op jit(solution)/shard_map/ppermute | solution.py:484
  24.2 3.4 %collective-permute-start.2 = (bf16[3,128,512]{2,1,0:T(8,128)(2,1)S(1)}, bf16[3,128,512]{2,1,0:T(8,128)(2,1)S(1)}, u32[]{:S(2)}, u32[]{:S(2)}) collective-permute-start(bf16[3,128,512]{2,1,0:T(8,128)(2,1)S(1)} %collective-permute-done.1.refs_1_), channel_id=1, source_target_pairs={{0,4},{1,5},{4,6},{5,7},{6,2},{7,3},{2,0},{3,1},{8,12},{9,13},{12,... | collective-permute-start | bytes 1179656 | tf_op jit(solution)/shard_map/ppermute | solution.py:484
  28.1 6.1 %collective-permute-done.2.refs_1_ = bf16[3,128,512]{2,1,0:T(8,128)(2,1)S(1)} collective-permute-done((bf16[3,128,512]{2,1,0:T(8,128)(2,1)S(1)}, bf16[3,128,512]{2,1,0:T(8,128)(2,1)S(1)}, u32[]{:S(2)}, u32[]{:S(2)}) %collective-permute-start.2) | collective-permute-done | bytes 393248 | tf_op jit(solution)/shard_map/ppermute | solution.py:484
  37.6 8.2 %attend_chunk_0.1 = (bf16[1,3,256,256]{3,2,1,0:T(8,128)(2,1)}, bf16[1,3,256,256]{3,2,1,0:T(8,128)(2,1)}, bf16[1,3,256,256]{3,2,1,0:T(8,128)(2,1)}, bf16[1,3,512,...) custom-call(s32[24]{0:T(128)} %concatenate.63.refs_0_.sp, ...), custom_call_target="tpu_custom_call" | custom-call | flops 600000000 | bytes 4000000 | tf_op jit(solution)/shard_map/attend_chunk_0/pallas_call | solution.py:376
  46.6 8.4 %attend_chunk_1.1 = (bf16[1,3,256,256]{3,2,1,0:T(8,128)(2,1)}, bf16[1,3,256,256]{3,2,1,0:T(8,128)(2,1)}, bf16[1,3,256,256]{3,2,1,0:T(8,128)(2,1)}, bf16[1,3,512,...) custom-call(s32[24]{0:T(128)} %concatenate.63.refs_0_.sp, ...), custom_call_target="tpu_custom_call" | custom-call | flops 600000000 | bytes 4000000 | tf_op jit(solution)/shard_map/attend_chunk_1/pallas_call | solution.py:376
  55.7 8.4 %attend_chunk_2.1 = (bf16[1,3,256,256]{3,2,1,0:T(8,128)(2,1)}, bf16[1,3,256,256]{3,2,1,0:T(8,128)(2,1)}, bf16[1,3,256,256]{3,2,1,0:T(8,128)(2,1)}, bf16[1,3,512,...) custom-call(s32[24]{0:T(128)} %concatenate.63.refs_0_.sp, ...), custom_call_target="tpu_custom_call" | custom-call | flops 600000000 | bytes 4000000 | tf_op jit(solution)/shard_map/attend_chunk_2/pallas_call | solution.py:376
  64.9 8.4 %attend_chunk_3.1 = (bf16[1,3,256,256]{3,2,1,0:T(8,128)(2,1)}, bf16[1,3,256,256]{3,2,1,0:T(8,128)(2,1)}, bf16[1,3,256,256]{3,2,1,0:T(8,128)(2,1)}, bf16[1,3,512,...) custom-call(s32[24]{0:T(128)} %concatenate.63.refs_0_.sp, ...), custom_call_target="tpu_custom_call" | custom-call | flops 600000000 | bytes 4000000 | tf_op jit(solution)/shard_map/attend_chunk_3/pallas_call | solution.py:376
  73.8 3.0 %pad_maximum_fusion.norm_t = bf16[4,3,512,256]{3,2,1,0:T(8,128)(2,1)} fusion(bf16[1,3,512,256]{3,2,1,0:T(8,128)(2,1)} %get-tuple-element.105, bf16[1,3,512,256]{3,2,1,0:T(8,128)(2,1)S(1)} %copy-done.14, bf16[1,3,512,256]{3,2,1,0:T(8,128)(2,1)S(1)} %copy-done.12, bf16[1,3,512,256]{3,2,1,0:T(8,128)(2,1)S(1)} %copy-done.10), kind=kLoop, calls=%fused_computation | loop fusion | flops 4718592 | bytes 6291456 | tf_op jit(solution)/shard_map/concatenate | solution.py:562
  79.4 10.2 %feed_forward.1 = (bf16[3,128,512]{2,1,0:T(8,128)(2,1)}, bf16[384,1024]{1,0:T(8,128)(2,1)}, bf16[384,1024]{1,0:T(8,128)(2,1)}, bf16[384,1024]{1,0:T(8,128)(2,1)}...) custom-call(s32[24]{0:T(128)} %concatenate.63.refs_0_.sp, ...), custom_call_target="tpu_custom_call" | custom-call | flops 4000000000 | bytes 10000000 | tf_op jit(solution)/shard_map/feed_forward/pallas_call | solution.py:376
  94.7 25.5 %attend_back.1 = (bf16[4,3,128,512]{3,2,1,0:T(8,128)(2,1)}, bf16[4,3,128,512]{3,2,1,0:T(8,128)(2,1)}, bf16[16,80,512]{2,1,0:T(8,128)(2,1)}) custom-call(s32[24]{0:T(128)} %concatenate.63.refs_0_.sp, bf16[3,128,512]{2,1,0:T(8,128)(2,1)} %get-tuple-element.86.br_m, bf16[3,128,512]{2,1,0:T(8,128)(2,1)} %copy-done.44, bf16[512,512]{1,0:T(8,128)(2,1)} %wo.1, ...), custom_call_target="tpu_custom_call" | custom-call | flops 8000000000 | bytes 10000000 | tf_op jit(solution)/shard_map/attend_back/pallas_call | solution.py:376
  127.7 3.4 %collective-permute-start.13 = (bf16[3,128,512]{2,1,0:T(8,128)(2,1)S(1)}, bf16[3,128,512]{2,1,0:T(8,128)(2,1)S(1)}, u32[]{:S(2)}, u32[]{:S(2)}) collective-permute-start(bf16[3,128,512]{2,1,0:T(8,128)(2,1)S(1)} %fusion), channel_id=1, source_target_pairs={{0,4},{1,5},{4,6},{5,7},{6,2},{7,3},{2,0},{3,1},{8,12},{9,13},{12,... | collective-permute-start | bytes 1179656 | tf_op jit(solution)/shard_map/ppermute | solution.py:596
  131.1 6.5 %feed_forward_grad.1 = (bf16[16,64,512]{2,1,0:T(8,128)(2,1)}, bf16[16,32,1024]{2,1,0:T(8,128)(2,1)}) custom-call(s32[24]{0:T(128)} %concatenate.63.refs_0_.sp, bf16[384,1024]{1,0:T(8,128)(2,1)} %get-tuple-element.117.hid_m, bf16[384,1024]{1,0:T(8,128)(2,1)} %copy-done.38, bf16[384,512]{1,0:T(8,128)(2,1)} %bitcast.71, bf16[384,512]{1,0:T(8,128)(2,1)} %bitcast.72, ...), custom_call_target="tpu_custom_call" | custom-call | flops 1600000000 | bytes 5000000 | tf_op jit(solution)/shard_map/feed_forward_grad/pallas_call | solution.py:376
  143.9 9.9 %collective-permute-done.29 = bf16[8,64,512]{2,1,0:T(8,128)(2,1)S(1)} collective-permute-done((bf16[8,64,512]{2,1,0:T(8,128)(2,1)S(1)}, bf16[8,64,512]{2,1,0:T(8,128)(2,1)S(1)}, u32[]{:S(2)}, u32[]{:S(2)}) %collective-permute-start.29) | collective-permute-done | bytes 524320 | tf_op jit(solution)/shard_map/ppermute | solution.py:402
  155.5 8.0 %collective-permute-done.17 = bf16[4,80,512]{2,1,0:T(8,128)(2,1)S(1)} collective-permute-done((bf16[4,80,512]{2,1,0:T(8,128)(2,1)S(1)}, bf16[4,80,512]{2,1,0:T(8,128)(2,1)S(1)}, u32[]{:S(2)}, u32[]{:S(2)}) %collective-permute-start.17) | collective-permute-done | bytes 327712 | tf_op jit(solution)/shard_map/ppermute | solution.py:402
  166.8 3.2 %collective-permute-done.18 = bf16[2,80,512]{2,1,0:T(8,128)(2,1)S(1)} collective-permute-done((bf16[2,80,512]{2,1,0:T(8,128)(2,1)S(1)}, bf16[2,80,512]{2,1,0:T(8,128)(2,1)S(1)}, u32[]{:S(2)}, u32[]{:S(2)}) %collective-permute-start.18) | collective-permute-done | bytes 163872 | tf_op jit(solution)/shard_map/ppermute | solution.py:402
  170.1 4.0 %collective-permute-start.19 = (bf16[1,80,512]{2,1,0:T(8,128)(2,1)S(1)}, bf16[1,80,512]{2,1,0:T(8,128)(2,1)S(1)}, u32[]{:S(2)}, u32[]{:S(2)}) collective-permute-start(bf16[1,80,512]{2,1,0:T(8,128)(2,1)S(1)} %slice.169), channel_id=1, source_target_pairs={{0,4},{1,5},{2,6},{3,7},{4,0},{5,1},{6,2},{7,3},{8,12},{9,13},{10,... | collective-permute-start | bytes 245768 | tf_op jit(solution)/shard_map/ppermute | solution.py:402
  174.3 2.8 %collective-permute-done.19 = bf16[1,80,512]{2,1,0:T(8,128)(2,1)S(1)} collective-permute-done((bf16[1,80,512]{2,1,0:T(8,128)(2,1)S(1)}, bf16[1,80,512]{2,1,0:T(8,128)(2,1)S(1)}, u32[]{:S(2)}, u32[]{:S(2)}) %collective-permute-start.19) | collective-permute-done | bytes 81952 | tf_op jit(solution)/shard_map/ppermute | solution.py:402
  179.8 5.8 %collective-permute-done.20 = bf16[1,80,512]{2,1,0:T(8,128)(2,1)S(1)} collective-permute-done((bf16[1,80,512]{2,1,0:T(8,128)(2,1)S(1)}, bf16[1,80,512]{2,1,0:T(8,128)(2,1)S(1)}, u32[]{:S(2)}, u32[]{:S(2)}) %collective-permute-start.20) | collective-permute-done | bytes 81952 | tf_op jit(solution)/shard_map/ppermute | solution.py:402
  185.7 2.6 collective-permute-start.32
  191.1 3.3 %collective-permute-start.33 = (bf16[1,64,512]{2,1,0:T(8,128)(2,1)S(1)}, bf16[1,64,512]{2,1,0:T(8,128)(2,1)S(1)}, u32[]{:S(2)}, u32[]{:S(2)}) collective-permute-start(bf16[1,64,512]{2,1,0:T(8,128)(2,1)S(1)} %get-tuple-element.130), channel_id=1, source_target_pairs={{0,4},{1,5},{2,6},{3,7},{4,0},{5,1},{6,2},{7,3},{8,12},{9,13},{10,... | collective-permute-start | bytes 196616 | tf_op jit(solution)/shard_map/ppermute | solution.py:402
  206.0 5.2 %collective-permute-done.22 = bf16[4,80,512]{2,1,0:T(8,128)(2,1)S(1)} collective-permute-done((bf16[4,80,512]{2,1,0:T(8,128)(2,1)S(1)}, bf16[4,80,512]{2,1,0:T(8,128)(2,1)S(1)}, u32[]{:S(2)}, u32[]{:S(2)}) %collective-permute-start.22) | collective-permute-done | bytes 327712 | tf_op jit(solution)/shard_map/ppermute | solution.py:402
  211.9 3.9 %collective-permute-done.35 = bf16[4,64,512]{2,1,0:T(8,128)(2,1)S(1)} collective-permute-done((bf16[4,64,512]{2,1,0:T(8,128)(2,1)S(1)}, bf16[4,64,512]{2,1,0:T(8,128)(2,1)S(1)}, u32[]{:S(2)}, u32[]{:S(2)}) %collective-permute-start.35) | collective-permute-done | bytes 262176 | tf_op jit(solution)/shard_map/ppermute | solution.py:402
  218.2 5.3 %collective-permute-done.23 = bf16[8,80,512]{2,1,0:T(8,128)(2,1)S(1)} collective-permute-done((bf16[8,80,512]{2,1,0:T(8,128)(2,1)S(1)}, bf16[8,80,512]{2,1,0:T(8,128)(2,1)S(1)}, u32[]{:S(2)}, u32[]{:S(2)}) %collective-permute-start.23) | collective-permute-done | bytes 655392 | tf_op jit(solution)/shard_map/ppermute | solution.py:402
  223.6 5.5 %collective-permute-done.36 = bf16[8,64,512]{2,1,0:T(8,128)(2,1)S(1)} collective-permute-done((bf16[8,64,512]{2,1,0:T(8,128)(2,1)S(1)}, bf16[8,64,512]{2,1,0:T(8,128)(2,1)S(1)}, u32[]{:S(2)}, u32[]{:S(2)}) %collective-permute-start.36) | collective-permute-done | bytes 524320 | tf_op jit(solution)/shard_map/ppermute | solution.py:402
  230.4 7.8 %collective-permute-done.14 = bf16[3,128,512]{2,1,0:T(8,128)(2,1)S(1)} collective-permute-done((bf16[3,128,512]{2,1,0:T(8,128)(2,1)S(1)}, bf16[3,128,512]{2,1,0:T(8,128)(2,1)S(1)}, u32[]{:S(2)}, u32[]{:S(2)}) %collective-permute-start.14) | collective-permute-done | bytes 393248 | tf_op jit(solution)/shard_map/ppermute | solution.py:596
  240.4 7.6 %collective-permute-done.15.arrived = bf16[3,128,512]{2,1,0:T(8,128)(2,1)S(1)} collective-permute-done((bf16[3,128,512]{2,1,0:T(8,128)(2,1)S(1)}, bf16[3,128,512]{2,1,0:T(8,128)(2,1)S(1)}, u32[]{:S(2)}, u32[]{:S(2)}) %collective-permute-start.15) | collective-permute-done | bytes 393248 | tf_op jit(solution)/shard_map/ppermute | solution.py:596
  248.8 2.8 %input_grad.1 = bf16[3,128,512]{2,1,0:T(8,128)(2,1)} custom-call(bf16[3,128,512]{2,1,0:T(8,128)(2,1)} %tokens.3, f32[1,512]{1,0:T(1,128)} %bitcast.52, f32[384,512]{1,0:T(8,128)} %get-tuple-element.85.mid_grad, bf16[3,128,512]{2,1,0:T(8,128)(2,1)} %get-tuple-element.134.own, bf16[3,128,512]{2,1,0:T(8,128)(2,1)} %copy-done.35), custom_call_target="tpu_custom_call" | custom-call | tf_op jit(solution)/shard_map/input_grad/pallas_call | solution.py:609
  252.6 6.8 %unpack_feed_forward.1 = (f32[2048,512]{1,0:T(8,128)}, f32[512,2048]{1,0:T(8,128)}) custom-call(s32[24]{0:T(128)} %concatenate.63.refs_0_.sp, bf16[16,64,512]{2,1,0:T(8,128)(2,1)} %copy-done.4, bf16[16,64,512]{2,1,0:T(8,128)(2,1)} %copy-done.6, bf16[16,32,1024]{2,1,0:T(8,128)(2,1)} %copy-done.5, bf16[16,32,1024]{2,1,0:T(8,128)(2,1)} %collective-permute-done.46.u_o), custom_call_target="tpu_custom_call" | custom-call | tf_op jit(solution)/shard_map/unpack_feed_forward/pallas_call | solution.py:376
  260.4 4.6 %unpack_attend.1 = (f32[512,512]{1,0:T(8,128)}, f32[512,512]{1,0:T(8,128)}, f32[512,512]{1,0:T(8,128)}, f32[512,512]{1,0:T(8,128)}, f32[16,512]{1,0:T(8,128)}) custom-call(s32[24]{0:T(128)} %concatenate.63.refs_0_.sp, bf16[16,80,512]{2,1,0:T(8,128)(2,1)} %copy-done.1, bf16[16,80,512]{2,1,0:T(8,128)(2,1)} %copy-done.3), custom_call_target="tpu_custom_call" | custom-call | tf_op jit(solution)/shard_map/unpack_attend/pallas_call | solution.py:376
  (223 shorter events, 62.6 us)
Async XLA Ops:
  0.7 12.8 %collective-permute-start = (bf16[3,128,512]{2,1,0:T(8,128)(2,1)}, bf16[3,128,512]{2,1,0:T(8,128)(2,1)S(1)}, u32[]{:S(2)}, u32[]{:S(2)}) collective-permute-start(bf16[3,128,512]{2,1,0:T(8,128)(2,1)} %tokens.3), channel_id=1, source_target_pairs={{0,4},{1,5},{4,6},{5,7},{6,2},{7,3},{2,0},{3,1},{8,12},{9,13},{12,... | collective-permute-start | bytes 1179656 | tf_op jit(solution)/shard_map/ppermute | solution.py:484
  13.4 10.8 %collective-permute-start.1 = (bf16[3,128,512]{2,1,0:T(8,128)(2,1)S(1)}, bf16[3,128,512]{2,1,0:T(8,128)(2,1)S(1)}, u32[]{:S(2)}, u32[]{:S(2)}) collective-permute-start(bf16[3,128,512]{2,1,0:T(8,128)(2,1)S(1)} %collective-permute-done.refs_1_), channel_id=1, source_target_pairs={{0,4},{1,5},{4,6},{5,7},{6,2},{7,3},{2,0},{3,1},{8,12},{9,13},{12,... | collective-permute-start | bytes 1179656 | tf_op jit(solution)/shard_map/ppermute | solution.py:484
  24.2 10.0 %collective-permute-start.2 = (bf16[3,128,512]{2,1,0:T(8,128)(2,1)S(1)}, bf16[3,128,512]{2,1,0:T(8,128)(2,1)S(1)}, u32[]{:S(2)}, u32[]{:S(2)}) collective-permute-start(bf16[3,128,512]{2,1,0:T(8,128)(2,1)S(1)} %collective-permute-done.1.refs_1_), channel_id=1, source_target_pairs={{0,4},{1,5},{4,6},{5,7},{6,2},{7,3},{2,0},{3,1},{8,12},{9,13},{12,... | collective-permute-start | bytes 1179656 | tf_op jit(solution)/shard_map/ppermute | solution.py:484
  27.6 9.3 %collective-permute-start.4 = (bf16[3,128,512]{2,1,0:T(8,128)(2,1)}, bf16[3,128,512]{2,1,0:T(8,128)(2,1)S(1)}, u32[]{:S(2)}, u32[]{:S(2)}) collective-permute-start(bf16[3,128,512]{2,1,0:T(8,128)(2,1)} %tokens.3), channel_id=1, source_target_pairs={{0,1},{1,0},{2,3},{3,2},{4,5},{5,4},{6,7},{7,6},{8,9},{9,8},{10,11... | collective-permute-start | bytes 1179656 | tf_op jit(solution)/shard_map/ppermute | solution.py:402
  27.6 18.2 %collective-permute-start.6 = (bf16[3,128,512]{2,1,0:T(8,128)(2,1)S(1)}, bf16[3,128,512]{2,1,0:T(8,128)(2,1)S(1)}, u32[]{:S(2)}, u32[]{:S(2)}) collective-permute-start(bf16[3,128,512]{2,1,0:T(8,128)(2,1)S(1)} %collective-permute-done.refs_1_), channel_id=1, source_target_pairs={{0,1},{1,0},{2,3},{3,2},{4,5},{5,4},{6,7},{7,6},{8,9},{9,8},{10,11... | collective-permute-start | bytes 1179656 | tf_op jit(solution)/shard_map/ppermute | solution.py:402
  28.1 26.9 %collective-permute-start.5 = (bf16[3,128,512]{2,1,0:T(8,128)(2,1)S(1)}, bf16[3,128,512]{2,1,0:T(8,128)(2,1)S(1)}, u32[]{:S(2)}, u32[]{:S(2)}) collective-permute-start(bf16[3,128,512]{2,1,0:T(8,128)(2,1)S(1)} %collective-permute-done.1.refs_1_), channel_id=1, source_target_pairs={{0,1},{1,0},{2,3},{3,2},{4,5},{5,4},{6,7},{7,6},{8,9},{9,8},{10,11... | collective-permute-start | bytes 1179656 | tf_op jit(solution)/shard_map/ppermute | solution.py:402
  34.2 29.9 %collective-permute-start.3 = (bf16[3,128,512]{2,1,0:T(8,128)(2,1)S(1)}, bf16[3,128,512]{2,1,0:T(8,128)(2,1)S(1)}, u32[]{:S(2)}, u32[]{:S(2)}) collective-permute-start(bf16[3,128,512]{2,1,0:T(8,128)(2,1)S(1)} %collective-permute-done.2.refs_1_), channel_id=1, source_target_pairs={{0,1},{1,0},{2,3},{3,2},{4,5},{5,4},{6,7},{7,6},{8,9},{9,8},{10,11... | collective-permute-start | bytes 1179656 | tf_op jit(solution)/shard_map/ppermute | solution.py:402
  123.0 16.8 %collective-permute-start.16 = (bf16[8,80,512]{2,1,0:T(8,128)(2,1)S(1)}, bf16[8,80,512]{2,1,0:T(8,128)(2,1)S(1)}, u32[]{:S(2)}, u32[]{:S(2)}) collective-permute-start(bf16[8,80,512]{2,1,0:T(8,128)(2,1)S(1)} %slice.132), channel_id=1, source_target_pairs={{0,8},{8,0},{16,24},{24,16},{1,9},{9,1},{17,25},{25,17},{2,10},{10... | collective-permute-start | bytes 1966088 | tf_op jit(solution)/shard_map/ppermute | solution.py:402
  126.6 15.0 %collective-permute-start.11 = (bf16[3,128,512]{2,1,0:T(8,128)(2,1)S(1)}, bf16[3,128,512]{2,1,0:T(8,128)(2,1)S(1)}, u32[]{:S(2)}, u32[]{:S(2)}) collective-permute-start(bf16[3,128,512]{2,1,0:T(8,128)(2,1)S(1)} %get-tuple-element.137), channel_id=1, source_target_pairs={{0,1},{1,0},{2,3},{3,2},{4,5},{5,4},{6,7},{7,6},{8,9},{9,8},{10,11... | collective-permute-start | bytes 1179656 | tf_op jit(solution)/shard_map/ppermute | solution.py:402
  127.1 102.7 %collective-permute-start.10 = (bf16[3,128,512]{2,1,0:T(8,128)(2,1)S(1)}, bf16[3,128,512]{2,1,0:T(8,128)(2,1)}, u32[]{:S(2)}, u32[]{:S(2)}) collective-permute-start(bf16[3,128,512]{2,1,0:T(8,128)(2,1)S(1)} %get-tuple-element.135), channel_id=1, source_target_pairs={{0,1},{1,0},{2,3},{3,2},{4,5},{5,4},{6,7},{7,6},{8,9},{9,8},{10,11... | collective-permute-start | bytes 1179656 | tf_op jit(solution)/shard_map/ppermute | solution.py:402
  127.5 102.9 %collective-permute-start.9 = (bf16[3,128,512]{2,1,0:T(8,128)(2,1)S(1)}, bf16[3,128,512]{2,1,0:T(8,128)(2,1)}, u32[]{:S(2)}, u32[]{:S(2)}) collective-permute-start(bf16[3,128,512]{2,1,0:T(8,128)(2,1)S(1)} %get-tuple-element.138), channel_id=1, source_target_pairs={{0,1},{1,0},{2,3},{3,2},{4,5},{5,4},{6,7},{7,6},{8,9},{9,8},{10,11... | collective-permute-start | bytes 1179656 | tf_op jit(solution)/shard_map/ppermute | solution.py:402
  127.7 15.5 %collective-permute-start.13 = (bf16[3,128,512]{2,1,0:T(8,128)(2,1)S(1)}, bf16[3,128,512]{2,1,0:T(8,128)(2,1)S(1)}, u32[]{:S(2)}, u32[]{:S(2)}) collective-permute-start(bf16[3,128,512]{2,1,0:T(8,128)(2,1)S(1)} %fusion), channel_id=1, source_target_pairs={{0,4},{1,5},{4,6},{5,7},{6,2},{7,3},{2,0},{3,1},{8,12},{9,13},{12,... | collective-permute-start | bytes 1179656 | tf_op jit(solution)/shard_map/ppermute | solution.py:596
  139.8 14.0 %collective-permute-start.29 = (bf16[8,64,512]{2,1,0:T(8,128)(2,1)S(1)}, bf16[8,64,512]{2,1,0:T(8,128)(2,1)S(1)}, u32[]{:S(2)}, u32[]{:S(2)}) collective-permute-start(bf16[8,64,512]{2,1,0:T(8,128)(2,1)S(1)} %slice.140), channel_id=1, source_target_pairs={{0,8},{8,0},{16,24},{24,16},{1,9},{9,1},{17,25},{25,17},{2,10},{10... | collective-permute-start | bytes 1572872 | tf_op jit(solution)/shard_map/ppermute | solution.py:402
  141.6 24.4 %collective-permute-start.38 = (bf16[8,32,1024]{2,1,0:T(8,128)(2,1)S(1)}, bf16[8,32,1024]{2,1,0:T(8,128)(2,1)S(1)}, u32[]{:S(2)}, u32[]{:S(2)}) collective-permute-start(bf16[8,32,1024]{2,1,0:T(8,128)(2,1)S(1)} %slice.148), channel_id=1, source_target_pairs={{0,16},{8,24},{16,0},{24,8},{1,17},{9,25},{17,1},{25,9},{2,18},{10... | collective-permute-start | bytes 1572872 | tf_op jit(solution)/shard_map/ppermute | solution.py:402
  143.2 20.3 %collective-permute-start.17 = (bf16[4,80,512]{2,1,0:T(8,128)(2,1)S(1)}, bf16[4,80,512]{2,1,0:T(8,128)(2,1)S(1)}, u32[]{:S(2)}, u32[]{:S(2)}) collective-permute-start(bf16[4,80,512]{2,1,0:T(8,128)(2,1)S(1)} %slice.165), channel_id=1, source_target_pairs={{0,16},{8,24},{16,0},{24,8},{1,17},{9,25},{17,1},{25,9},{2,18},{10... | collective-permute-start | bytes 983048 | tf_op jit(solution)/shard_map/ppermute | solution.py:402
  154.0 20.1 %collective-permute-start.30 = (bf16[4,64,512]{2,1,0:T(8,128)(2,1)S(1)}, bf16[4,64,512]{2,1,0:T(8,128)(2,1)S(1)}, u32[]{:S(2)}, u32[]{:S(2)}) collective-permute-start(bf16[4,64,512]{2,1,0:T(8,128)(2,1)S(1)} %slice.171), channel_id=1, source_target_pairs={{0,16},{8,24},{16,0},{24,8},{1,17},{9,25},{17,1},{25,9},{2,18},{10... | collective-permute-start | bytes 786440 | tf_op jit(solution)/shard_map/ppermute | solution.py:402
  166.2 13.3 %collective-permute-start.39 = (bf16[4,32,1024]{2,1,0:T(8,128)(2,1)S(1)}, bf16[4,32,1024]{2,1,0:T(8,128)(2,1)S(1)}, u32[]{:S(2)}, u32[]{:S(2)}) collective-permute-start(bf16[4,32,1024]{2,1,0:T(8,128)(2,1)S(1)} %slice.177), channel_id=1, source_target_pairs={{0,8},{8,0},{16,24},{24,16},{1,9},{9,1},{17,25},{25,17},{2,10},{10... | collective-permute-start | bytes 786440 | tf_op jit(solution)/shard_map/ppermute | solution.py:402
  174.2 11.5 %collective-permute-start.31 = (bf16[2,64,512]{2,1,0:T(8,128)(2,1)S(1)}, bf16[2,64,512]{2,1,0:T(8,128)(2,1)S(1)}, u32[]{:S(2)}, u32[]{:S(2)}) collective-permute-start(bf16[2,64,512]{2,1,0:T(8,128)(2,1)S(1)} %slice.173), channel_id=1, source_target_pairs={{0,2},{1,3},{2,0},{3,1},{4,6},{5,7},{6,4},{7,5},{8,10},{9,11},{10,... | collective-permute-start | bytes 393224 | tf_op jit(solution)/shard_map/ppermute | solution.py:402
  177.2 8.4 %collective-permute-start.20 = (bf16[1,80,512]{2,1,0:T(8,128)(2,1)S(1)}, bf16[1,80,512]{2,1,0:T(8,128)(2,1)S(1)}, u32[]{:S(2)}, u32[]{:S(2)}) collective-permute-start(bf16[1,80,512]{2,1,0:T(8,128)(2,1)S(1)} %get-tuple-element.132), channel_id=1, source_target_pairs={{0,4},{1,5},{2,6},{3,7},{4,0},{5,1},{6,2},{7,3},{8,12},{9,13},{10,... | collective-permute-start | bytes 245768 | tf_op jit(solution)/shard_map/ppermute | solution.py:402
  179.6 8.8 %collective-permute-start.40 = (bf16[2,32,1024]{2,1,0:T(8,128)(2,1)S(1)}, bf16[2,32,1024]{2,1,0:T(8,128)(2,1)S(1)}, u32[]{:S(2)}, u32[]{:S(2)}) collective-permute-start(bf16[2,32,1024]{2,1,0:T(8,128)(2,1)S(1)} %slice.179), channel_id=1, source_target_pairs={{0,2},{1,3},{2,0},{3,1},{4,6},{5,7},{6,4},{7,5},{8,10},{9,11},{10,... | collective-permute-start | bytes 393224 | tf_op jit(solution)/shard_map/ppermute | solution.py:402
  185.6 15.0 %collective-permute-start.21 = (bf16[2,80,512]{2,1,0:T(8,128)(2,1)S(1)}, bf16[2,80,512]{2,1,0:T(8,128)(2,1)S(1)}, u32[]{:S(2)}, u32[]{:S(2)}) collective-permute-start(bf16[2,80,512]{2,1,0:T(8,128)(2,1)S(1)} %pad_maximum_fusion.11), channel_id=1, source_target_pairs={{0,2},{1,3},{2,0},{3,1},{4,6},{5,7},{6,4},{7,5},{8,10},{9,11},{10,... | collective-permute-start | bytes 491528 | tf_op jit(solution)/shard_map/ppermute | solution.py:402
  200.6 10.6 %collective-permute-start.22 = (bf16[4,80,512]{2,1,0:T(8,128)(2,1)S(1)}, bf16[4,80,512]{2,1,0:T(8,128)(2,1)S(1)}, u32[]{:S(2)}, u32[]{:S(2)}) collective-permute-start(bf16[4,80,512]{2,1,0:T(8,128)(2,1)S(1)} %pad_maximum_fusion.8), channel_id=1, source_target_pairs={{0,16},{8,24},{16,0},{24,8},{1,17},{9,25},{17,1},{25,9},{2,18},{10... | collective-permute-start | bytes 983048 | tf_op jit(solution)/shard_map/ppermute | solution.py:402
  202.3 13.5 %collective-permute-start.35 = (bf16[4,64,512]{2,1,0:T(8,128)(2,1)S(1)}, bf16[4,64,512]{2,1,0:T(8,128)(2,1)S(1)}, u32[]{:S(2)}, u32[]{:S(2)}) collective-permute-start(bf16[4,64,512]{2,1,0:T(8,128)(2,1)S(1)} %pad_maximum_fusion.9), channel_id=1, source_target_pairs={{0,16},{8,24},{16,0},{24,8},{1,17},{9,25},{17,1},{25,9},{2,18},{10... | collective-permute-start | bytes 786440 | tf_op jit(solution)/shard_map/ppermute | solution.py:402
  205.4 11.0 %collective-permute-start.44 = (bf16[4,32,1024]{2,1,0:T(8,128)(2,1)S(1)}, bf16[4,32,1024]{2,1,0:T(8,128)(2,1)S(1)}, u32[]{:S(2)}, u32[]{:S(2)}) collective-permute-start(bf16[4,32,1024]{2,1,0:T(8,128)(2,1)S(1)} %pad_maximum_fusion.10), channel_id=1, source_target_pairs={{0,8},{8,0},{16,24},{24,16},{1,9},{9,1},{17,25},{25,17},{2,10},{10... | collective-permute-start | bytes 786440 | tf_op jit(solution)/shard_map/ppermute | solution.py:402
  211.3 12.2 %collective-permute-start.23 = (bf16[8,80,512]{2,1,0:T(8,128)(2,1)S(1)}, bf16[8,80,512]{2,1,0:T(8,128)(2,1)S(1)}, u32[]{:S(2)}, u32[]{:S(2)}) collective-permute-start(bf16[8,80,512]{2,1,0:T(8,128)(2,1)S(1)} %pad_maximum_fusion.5), channel_id=1, source_target_pairs={{0,8},{8,0},{16,24},{24,16},{1,9},{9,1},{17,25},{25,17},{2,10},{10... | collective-permute-start | bytes 1966088 | tf_op jit(solution)/shard_map/ppermute | solution.py:402
  215.8 13.3 %collective-permute-start.36 = (bf16[8,64,512]{2,1,0:T(8,128)(2,1)S(1)}, bf16[8,64,512]{2,1,0:T(8,128)(2,1)S(1)}, u32[]{:S(2)}, u32[]{:S(2)}) collective-permute-start(bf16[8,64,512]{2,1,0:T(8,128)(2,1)S(1)} %pad_maximum_fusion.6), channel_id=1, source_target_pairs={{0,8},{8,0},{16,24},{24,16},{1,9},{9,1},{17,25},{25,17},{2,10},{10... | collective-permute-start | bytes 1572872 | tf_op jit(solution)/shard_map/ppermute | solution.py:402
  216.5 13.2 %collective-permute-start.45 = (bf16[8,32,1024]{2,1,0:T(8,128)(2,1)S(1)}, bf16[8,32,1024]{2,1,0:T(8,128)(2,1)S(1)}, u32[]{:S(2)}, u32[]{:S(2)}) collective-permute-start(bf16[8,32,1024]{2,1,0:T(8,128)(2,1)S(1)} %pad_maximum_fusion.7), channel_id=1, source_target_pairs={{0,16},{8,24},{16,0},{24,8},{1,17},{9,25},{17,1},{25,9},{2,18},{10... | collective-permute-start | bytes 1572872 | tf_op jit(solution)/shard_map/ppermute | solution.py:402
  223.5 35.8 %collective-permute-start.24 = (bf16[16,80,512]{2,1,0:T(8,128)(2,1)S(1)}, bf16[16,80,512]{2,1,0:T(8,128)(2,1)S(1)}, u32[]{:S(2)}, u32[]{:S(2)}) collective-permute-start(bf16[16,80,512]{2,1,0:T(8,128)(2,1)S(1)} %constant_dynamic-update-slice_fusion.a_m), channel_id=1, source_target_pairs={{0,1},{1,0},{2,3},{3,2},{4,5},{5,4},{6,7},{7,6},{8,9},{9,8},{10,11... | collective-permute-start | bytes 3932168 | tf_op jit(solution)/shard_map/ppermute | solution.py:402
  229.1 9.0 %collective-permute-start.14 = (bf16[3,128,512]{2,1,0:T(8,128)(2,1)S(1)}, bf16[3,128,512]{2,1,0:T(8,128)(2,1)S(1)}, u32[]{:S(2)}, u32[]{:S(2)}) collective-permute-start(bf16[3,128,512]{2,1,0:T(8,128)(2,1)S(1)} %fusion.2), channel_id=1, source_target_pairs={{0,4},{1,5},{4,6},{5,7},{6,2},{7,3},{2,0},{3,1},{8,12},{9,13},{12,... | collective-permute-start | bytes 1179656 | tf_op jit(solution)/shard_map/ppermute | solution.py:596
  229.7 21.9 %collective-permute-start.37 = (bf16[16,64,512]{2,1,0:T(8,128)(2,1)S(1)}, bf16[16,64,512]{2,1,0:T(8,128)(2,1)S(1)}, u32[]{:S(2)}, u32[]{:S(2)}) collective-permute-start(bf16[16,64,512]{2,1,0:T(8,128)(2,1)S(1)} %constant_dynamic-update-slice_fusion.5.d_m), channel_id=1, source_target_pairs={{0,1},{1,0},{2,3},{3,2},{4,5},{5,4},{6,7},{7,6},{8,9},{9,8},{10,11... | collective-permute-start | bytes 3145736 | tf_op jit(solution)/shard_map/ppermute | solution.py:402
  229.8 21.8 %collective-permute-start.46 = (bf16[16,32,1024]{2,1,0:T(8,128)(2,1)S(1)}, bf16[16,32,1024]{2,1,0:T(8,128)(2,1)}, u32[]{:S(2)}, u32[]{:S(2)}) collective-permute-start(bf16[16,32,1024]{2,1,0:T(8,128)(2,1)S(1)} %constant_dynamic-update-slice_fusion.10.u_m), channel_id=1, source_target_pairs={{0,1},{1,0},{2,3},{3,2},{4,5},{5,4},{6,7},{7,6},{8,9},{9,8},{10,11... | collective-permute-start | bytes 3145736 | tf_op jit(solution)/shard_map/ppermute | solution.py:402
  240.3 7.8 %collective-permute-start.15 = (bf16[3,128,512]{2,1,0:T(8,128)(2,1)S(1)}, bf16[3,128,512]{2,1,0:T(8,128)(2,1)S(1)}, u32[]{:S(2)}, u32[]{:S(2)}) collective-permute-start(bf16[3,128,512]{2,1,0:T(8,128)(2,1)S(1)} %get-tuple-element.133), channel_id=1, source_target_pairs={{0,4},{1,5},{4,6},{5,7},{6,2},{7,3},{2,0},{3,1},{8,12},{9,13},{12,... | collective-permute-start | bytes 1179656 | tf_op jit(solution)/shard_map/ppermute | solution.py:596
  (61 other events, 430.5 us)
